TPU v7x, 32 devices: a whole 2x2x4 slice. The times are simulated.
32 devices in a mesh: dp: 16 (over z, y, x), tensor: 2 (over core).
Axes of the slice: x: 2, y: 2, z: 4, core: 2. Of those that a mesh axis runs over, the one named last changes fastest.
Arguments:
- tokens: bfloat16 [32, 1024, 512], P('dp', 'tensor'), may hold values from -6 to 6
- memory: bfloat16 [32, 1024, 512], P('dp', 'tensor'), may hold values from -6 to 6
- dec_segment: int32 [32, 1024], P('dp'), may hold values from 0 to 3, as said below
- enc_segment: int32 [32, 1024], P('dp'), may hold values from 0 to 3, as said below
- slot_left: int32 [32, 512], P('dp'), may hold values from 0 to 1022
- self_qkv: bfloat16 [3, 512, 512], P(None, None, 'tensor'), may hold values from -0.25 to 0.25
- self_bias: bfloat16 [2, 512], P(None, 'tensor'), may hold values from -3 to 3
- self_out: bfloat16 [512, 512], P('tensor'), may hold values from -4 to 4
- self_out_bias: bfloat16 [512], replicated, may hold values from -3 to 3
- cross_qkv: bfloat16 [3, 512, 512], P(None, None, 'tensor'), may hold values from -0.25 to 0.25
- cross_bias: bfloat16 [2, 512], P(None, 'tensor'), may hold values from -3 to 3
- cross_out: bfloat16 [512, 512], P('tensor'), may hold values from -4 to 4
- cross_out_bias: bfloat16 [512], replicated, may hold values from -3 to 3
- ffn_in: bfloat16 [512, 2048], P(None, 'tensor'), may hold values from -0.25 to 0.25
- ffn_in_bias: bfloat16 [2048], P('tensor'), may hold values from -3 to 3
- ffn_out: bfloat16 [2048, 512], P('tensor'), may hold values from -0.125 to 0.125
- ffn_out_bias: bfloat16 [512], replicated, may hold values from -3 to 3
- norm_gain: bfloat16 [3, 512], replicated, may hold values from 0.5 to 1.5
- norm_bias: bfloat16 [3, 512], replicated, may hold values from -2 to 2
- slot_weight: bfloat16 [1024, 512], P(None, 'tensor'), may hold values from -0.1875 to 0.1875
- slot_bias: bfloat16 [512], P('tensor'), may hold values from -3 to 3
- grad_output: bfloat16 [32, 1024, 512], P('dp', 'tensor'), may hold values from -6 to 6
- grad_slots: bfloat16 [32, 512, 512], P('dp', None, 'tensor'), may hold values from -6 to 6
Outputs:
- output: bfloat16 [32, 1024, 512], P('dp', 'tensor')
- slot_states: bfloat16 [32, 512, 512], P('dp', None, 'tensor')
- grad_input: bfloat16 [32, 1024, 512], P('dp', 'tensor')
- grad_memory: bfloat16 [32, 1024, 512], P('dp', 'tensor')
- grad_self_qkv: float32 [3, 512, 512], P(None, None, 'tensor')
- grad_self_bias: float32 [2, 512], P(None, 'tensor')
- grad_self_out: float32 [512, 512], P('tensor')
- grad_self_out_bias: float32 [512], replicated
- grad_cross_qkv: float32 [3, 512, 512], P(None, None, 'tensor')
- grad_cross_bias: float32 [2, 512], P(None, 'tensor')
- grad_cross_out: float32 [512, 512], P('tensor')
- grad_cross_out_bias: float32 [512], replicated
- grad_ffn_in: float32 [512, 2048], P(None, 'tensor')
- grad_ffn_in_bias: float32 [2048], P('tensor')
- grad_ffn_out: float32 [2048, 512], P('tensor')
- grad_ffn_out_bias: float32 [512], replicated
- grad_norm_gain: float32 [3, 512], replicated
- grad_norm_bias: float32 [3, 512], replicated
- grad_slot_weight: float32 [1024, 512], P(None, 'tensor')
- grad_slot_bias: float32 [512], P('tensor')
Inputs may be any that keep to these rules, and one draw needn't show every extreme that they name: `dec_segment`: within a row the ids never fall, and each of the 4 documents has at least one decoder token and at least one encoder token in that row. `enc_segment`: within a row the ids never fall; the documents are those of dec_segment in the same row. Slot j of row r pairs the states at positions slot_left[r, j] and slot_left[r, j] + 1 of that row.
All inputs are finite; a program needn't handle non-finite values.
Results may differ from a plain program's by a relative error of at most 0.023.
Values may be sent and summed in bfloat16 or wider, within the bound.
No kernel may reach another device: no remote copies, remote signals or barrier semaphores. Data moves between devices by JAX's collectives and lax.ppermute only.
A program may use at most 192 MiB of HBM per device.

v0:
```python
import functools
import math

import jax
import jax.numpy as jnp
from jax import lax
from jax.experimental import pallas as pl
from jax.experimental.pallas import tpu as pltpu
from jax.sharding import PartitionSpec as P

HEAD_DIM = 64
EPSILON = 1e-05
MASKED = -1e30
GELU_C = 0.7978845608028654
GELU_A = 0.044715
LOG2E = 1.4426950408889634
LN2 = 0.6931471805599453
SCALE = HEAD_DIM ** (-0.5)
AUG = 80
QB = 256
FWD_QB = 1024
FWD_HEADS = 4
FFN_TB = 512
TB = 256
VMEM_LIMIT = 63 * 2**20
SPARE = 20 * 2**20

bf16 = jnp.bfloat16
f32 = jnp.float32


def dg(a, b, ca, cb):
    return lax.dot_general(a, b, (((ca,), (cb,)), ((), ())), preferred_element_type=f32)


def column_of(row):
    return jnp.broadcast_to(row.astype(f32), (8, row.shape[1])).T[:, 0:1]


def three_parts(row):
    high = row.astype(bf16).astype(f32)
    rest = row - high
    middle = rest.astype(bf16).astype(f32)
    return high, middle, (rest - middle)


def tall(shape, rows):
    index = lax.broadcasted_iota(jnp.int32, shape, 0)
    block = jnp.zeros(shape, f32)
    for at, row in rows.items():
        block = jnp.where(index == at, jnp.broadcast_to(row, shape), block)
    return block


def norm_parts(y):
    centre = y - jnp.mean(y, axis=-1, keepdims=True)
    spread = lax.rsqrt(jnp.mean(centre * centre, axis=-1, keepdims=True) + EPSILON)
    return centre * spread, spread


def norm_back(xhat, spread, gain, e):
    a = e * gain
    dy = (a - jnp.mean(a, axis=-1, keepdims=True) - xhat * jnp.mean(a * xhat, axis=-1, keepdims=True)) * spread
    return dy, jnp.sum(e * xhat, axis=0, keepdims=True), jnp.sum(e, axis=0, keepdims=True)


ANY = pl.BlockSpec(memory_space=pl.ANY)
HBM = pl.BlockSpec(memory_space=pltpu.HBM)
VMEM = pl.BlockSpec(memory_space=pltpu.VMEM)
SMEM = pl.BlockSpec(memory_space=pltpu.SMEM)


class Staged:
    def __init__(self, far, near, sems, first, pick=None):
        self.far, self.near, self.sems, self.next, self.pending, self.pick = far, near, sems, first, [], pick

    def load(self):
        source = self.far if self.pick is None else self.far.at[self.pick]
        copy = pltpu.make_async_copy(source, self.near, self.sems.at[self.next])
        copy.start()
        self.pending.append(copy)

    def store(self, rows=None):
        near, far = (self.near, self.far) if rows is None else (self.near.at[rows], self.far.at[rows])
        copy = pltpu.make_async_copy(near, far, self.sems.at[self.next])
        self.next += 1
        copy.start()
        self.pending.append(copy)

    def wait(self):
        for copy in self.pending:
            copy.wait()
        self.pending = []
        return self.near


def staged_call(body, scalars, big_ins, small_ins, outs, small_outs=(), scratch=(), after=(), micros=10.0):
    def shape_of(a, part):
        if part is None:
            return a.shape
        return a.shape[1:] if part == "core" else (part.stop - part.start,) + a.shape[1:]

    def kernel(*refs):
        refs = list(refs)
        take = lambda n: [refs.pop(0) for _ in range(n)]
        (scalar_ref,) = take(1)
        far_in, smalls, _, far_out = take(len(big_ins)), take(len(small_ins)), take(len(after)), take(len(outs))
        short_out, buf_in, buf_out = take(len(small_outs)), take(len(big_ins)), take(len(outs))
        sem_in, sem_out = take(2)
        me = [scalar_ref[i] for i in range(scalars.shape[0])]
        ins = [
            Staged(far, near, sem_in, i, me[0] if part == "core" else part)
            for i, (far, near, (_, part)) in enumerate(zip(far_in, buf_in, big_ins))
        ]
        for one in ins:
            one.load()
        first = 0
        results = []
        for far, near, (_, _, n) in zip(far_out, buf_out, outs):
            results.append(Staged(far, near, sem_out, first))
            first += n
        body(me if len(me) > 1 else me[0], ins, smalls, results, short_out, refs)
        for one in ins + results:
            one.wait()

    held = [(shape_of(a, part), a.dtype) for a, part in big_ins] + [(s, d) for s, d, _ in outs]
    held += [(one.shape, one.dtype) for one in scratch]
    size = sum(math.prod(s) * jnp.dtype(d).itemsize for s, d in held)
    far = [pltpu.with_memory_space_constraint(a, pltpu.HBM) for a, _ in big_ins]
    small_ins = [pltpu.with_memory_space_constraint(a, pltpu.HBM) for a in small_ins]
    return pl.pallas_call(
        kernel,
        out_shape=[pltpu.HBM(s, d) for s, d, _ in outs] + [jax.ShapeDtypeStruct(s, d) for s, d in small_outs],
        in_specs=[SMEM] + [HBM] * len(big_ins) + [VMEM] * len(small_ins) + [ANY] * len(after),
        out_specs=[HBM] * len(outs) + [VMEM] * len(small_outs),
        scratch_shapes=[pltpu.VMEM(shape_of(a, part), a.dtype) for a, part in big_ins]
        + [pltpu.VMEM(s, d) for s, d, _ in outs]
        + [pltpu.SemaphoreType.DMA((len(big_ins),)), pltpu.SemaphoreType.DMA((max(1, sum(o[2] for o in outs)),))]
        + list(scratch),
        compiler_params=pltpu.CompilerParams(vmem_limit_bytes=min(VMEM_LIMIT, size + SPARE)),
        cost_estimate=pl.CostEstimate(flops=int(micros * 1.1e9), bytes_accessed=1024, transcendentals=0),
    )(scalars, *far, *small_ins, *after)


def row_of(ref):
    return ref[...].astype(f32).reshape(1, ref.shape[0])


S_GAIN, S_SHIFT, S_SELF_OB, S_CROSS_OB, S_FFN_OB, S_SELF_B, S_CROSS_B, S_FFN_B, S_SLOT_B = 0, 3, 6, 7, 8, 9, 10, 11, 13


def own_first(row, core):
    half = row.shape[1] // 2
    return jnp.where(core == 0, row, jnp.concatenate([row[:, half:], row[:, :half]], axis=1))


def attend_forward(cross, core, ins, smalls, outs, _, scratch):
    qa_s, ka_s, va_s, ctx_s, y_s, h_s = outs
    qa, ka, va, ctx, y_out, h_out = [o.near for o in outs]
    if cross:
        src_s, k_m, k_t, w_m, w_t, wo_m, wo_t = ins
        bias_m, bias_t, out_bias, gains, shifts, seg_d, seg_e = smalls
    else:
        k_m, k_t, w_m, w_t, wo_m, wo_t = ins
        bias_m, bias_t, out_bias, gains, shifts, seg_d = smalls
        seg_e = seg_d
    heads, _, length = qa.shape
    half = length // 2
    hw = w_m.near.shape[2]
    heads_half = heads // 2
    seg_q = own_first(seg_d[pl.ds(core, 1), :], core)
    seg_k = own_first(seg_e[pl.ds(core, 1), :], core)
    shape16 = (16, length)
    index = lax.broadcasted_iota(jnp.int32, shape16, 0)
    same_q = index == jnp.broadcast_to(seg_q, shape16)
    same_k = index == jnp.broadcast_to(seg_k, shape16)
    q_extra = jnp.where(index < 4, jnp.where(same_q, 0.0, MASKED), 0.0).astype(bf16)
    k_extra = jnp.where(index < 4, jnp.where(same_k, 1.0, 0.0), jnp.where(index < 7, 1.0, 0.0)).astype(bf16)
    v_extra = jnp.where(index < 3, 1.0, 0.0).astype(bf16)
    for h in range(heads):
        qa[h, 64:80, :] = q_extra
        ka[h, 64:80, :] = k_extra
        va[h, 64:80, :] = v_extra
    src_k = [k_m.wait(), k_t.wait()]
    if cross:
        src = src_s.wait()
        src_q = [src.at[0:half], src.at[half:length]]
    else:
        src_q = src_k
    for side, (w_s, short) in enumerate(((w_m, bias_m), (w_t, bias_t))):
        w = w_s.wait()
        bias_q = column_of(short[0:1, :])
        bias_v = column_of(short[1:2, :])
        for piece in range(2):
            at = slice(piece * half, (piece + 1) * half)
            q = ((dg(w[0], src_q[piece][...], 0, 1) + bias_q) * (SCALE * LOG2E)).astype(bf16)
            k = dg(w[1], src_k[piece][...], 0, 1).astype(bf16)
            v = (dg(w[2], src_k[piece][...], 0, 1) + bias_v).astype(bf16)
            for i in range(heads_half):
                h = side * heads_half + i
                rows = slice(i * HEAD_DIM, (i + 1) * HEAD_DIM)
                qa[h, 0:64, at] = q[rows]
                ka[h, 0:64, at] = k[rows]
                va[h, 0:64, at] = v[rows]
    ka_s.store()
    va_s.store()

    def some_heads(step, _):
        items = [(step * FWD_HEADS + j, slice(i, i + FWD_QB)) for j in range(FWD_HEADS) for i in range(0, length, FWD_QB)]

        def scores_of(item):
            h, at = item
            return dg(ka[h], qa[h, :, at], 0, 0)

        scores = scores_of(items[0])
        for n, (h, at) in enumerate(items):
            following = scores_of(items[n + 1]) if n + 1 < len(items) else None
            top = jnp.max(scores, axis=0, keepdims=True)
            weights = jnp.exp2(scores - top).astype(bf16)
            out = dg(va[h], weights, 1, 0)
            total = out[64:65, :]
            ctx[pl.ds(pl.multiple_of(h * HEAD_DIM, HEAD_DIM), HEAD_DIM), at] = (out[0:64, :] * (1.0 / total)).astype(bf16)
            high, middle, low = three_parts(-(top + jnp.log2(total)))
            extra = tall((16, FWD_QB), {4: high, 5: middle, 6: low})
            qa[h, 64:80, at] = qa[h, 64:80, at] + extra.astype(bf16)
            scores = following
        return 0

    lax.fori_loop(0, heads // FWD_HEADS, some_heads, 0)
    qa_s.store()
    ctx_s.store()
    norm = 1 if cross else 0
    bias = row_of(out_bias)
    gain = gains[norm : norm + 1, :].astype(f32)
    shift = shifts[norm : norm + 1, :].astype(f32)
    wo = [wo_m.wait(), wo_t.wait()]
    for i in range(length // TB):
        at = slice(i * TB, (i + 1) * TB)
        y = dg(ctx[0:hw, at], wo[0][...], 0, 0) + dg(ctx[hw:, at], wo[1][...], 0, 0) + bias
        piece, inner = divmod(i * TB, half)
        y = y + src_q[piece][inner : inner + TB, :].astype(f32)
        y_out[at, :] = y
        y_s.store(at)
        xhat, _ = norm_parts(y)
        h_out[at, :] = (xhat * gain + shift).astype(bf16)
        h_s.store(at)


def back_heads(count, qa, ka, va, da, ctx, dq, dk, dv):
    length = qa.shape[2]

    def one_head(h, _):
        rows = pl.ds(pl.multiple_of(h * HEAD_DIM, HEAD_DIM), HEAD_DIM)
        keys = ka[h]
        values = va[h]
        inner = jnp.sum(da[h, 0:64, :].astype(f32) * ctx[rows, :].astype(f32), axis=0, keepdims=True)
        high, middle, low = three_parts(-inner)
        da[h, 64:80, :] = tall((16, length), {0: high, 1: middle, 2: low}).astype(bf16)
        cuts = [slice(i * QB, (i + 1) * QB) for i in range(length // QB)]

        def products(at):
            return dg(qa[h, :, at], keys, 0, 0), dg(da[h, :, at], values, 0, 0)

        ahead = products(cuts[0])
        for n, at in enumerate(cuts):
            scores, spread = ahead
            if n + 1 < len(cuts):
                ahead = products(cuts[n + 1])
            weights = jnp.exp2(scores)
            ds = (weights * spread).astype(bf16)
            dv_part = dg(da[h, 0:64, at], weights.astype(bf16), 1, 0)
            dk_part = dg(qa[h, 0:64, at], ds, 1, 0)
            dv_sum = dv_part if n == 0 else dv_sum + dv_part
            dk_sum = dk_part if n == 0 else dk_sum + dk_part
            dq[rows, at] = (dg(keys[0:64], ds, 1, 1) * SCALE).astype(bf16)
        dk[rows, :] = (dk_sum * LN2).astype(bf16)
        dv[rows, :] = dv_sum.astype(bf16)
        return 0

    lax.fori_loop(0, count, one_head, 0)


def weight_rows(g, grads, sources):
    for j, (grad, pair) in enumerate(zip(grads, sources)):
        hw, length = grad.shape
        half = length // 2
        total = dg(pair[0][...], grad[:, 0:half], 0, 1) + dg(pair[1][...], grad[:, half:length], 0, 1)
        put = slice(j * hw, (j + 1) * hw)
        inner = total.shape[0] // 2
        g.near[put, 0:hw] = total[0:inner].astype(bf16)
        g.near[put, hw : 2 * hw] = total[inner:].astype(bf16)
        g.store(put)


def position_sums(dq, dv):
    ones = jnp.ones((8, dq.shape[1]), bf16)
    return dg(ones, dq[...], 1, 1)[0:1], dg(ones, dv[...], 1, 1)[0:1]


def heads_backward(ins, outs, da, dout):
    wo, ctx, va, qa, ka = ins
    dctx = dg(wo.wait()[...], dout[...], 1, 1).astype(bf16)
    for i in range(da.shape[0]):
        da[i, 0:64, :] = dctx[i * HEAD_DIM : (i + 1) * HEAD_DIM]
    ctx, va, qa, ka = ctx.wait(), va.wait(), qa.wait(), ka.wait()
    grads = [one.near for one in outs]
    back_heads(qa.shape[0], qa, ka, va, da, ctx, *grads)
    for one in outs:
        one.store()
    return grads


def halves_of(staged):
    if len(staged) == 2:
        return [one.wait() for one in staged]
    whole = staged[0].wait()
    half = whole.shape[0] // 2
    return [whole.at[0:half], whole.at[half : 2 * half]]


def out_rows(g, ctx, dout):
    hw = ctx.shape[0]
    put = slice(3 * hw, 4 * hw)
    g.near[put, :] = dg(ctx[...], dout[...], 1, 0).astype(bf16)
    g.store(put)


def cross_backward_first(core, ins, smalls, outs, _, scratch):
    do_s, src_s, k_m, k_t = ins[0:4]
    short, = smalls
    g, ns = outs[0:2]
    dout = do_s.wait()
    grads = heads_backward(ins[4:9], outs[2:5], scratch[0], dout)
    out_rows(g, ins[5].near, dout)
    src_k = [k_m.wait(), k_t.wait()]
    weight_rows(g, grads, [halves_of([src_s]), src_k, src_k])
    q_sum, v_sum = position_sums(grads[0], grads[2])
    ns.near[...] = short[...]
    ns.near[S_CROSS_B : S_CROSS_B + 1, :] = jnp.concatenate([q_sum, v_sum], axis=1)
    ns.store()


def cross_backward_second(core, ins, smalls, outs, _, scratch):
    do_s, src_s, k_m, k_t = ins[0:4]
    dy_s, y_s, dqt_s, wq_m, wq_t, ctx1_s = ins[9:15]
    gains, short_m, short_t = smalls
    g, ns_m, ns_t = outs[0:3]
    dprev_s, do1_s, so_t = outs[6:9]
    dout = do_s.wait()
    grads = heads_backward(ins[4:9], outs[3:6], scratch[0], dout)
    dq_m = grads[0]
    dq_t = dqt_s.wait()
    w = [wq_m.wait(), wq_t.wait()]
    y_prev = y_s.wait()
    dy = dy_s.wait()
    length, width = dy.shape
    hw = dq_m.shape[0]
    dprev = dprev_s.near
    dout1 = do1_s.near
    gain = gains[0:1, :].astype(f32)
    gain_sum = jnp.zeros((1, width), f32)
    shift_sum = jnp.zeros((1, width), f32)
    out_sum = jnp.zeros((1, width), f32)
    for i in range(length // TB):
        at = slice(i * TB, (i + 1) * TB)
        e = dy[at, :] + dg(dq_m[:, at], w[0][0], 0, 1) + dg(dq_t[:, at], w[1][0], 0, 1)
        xhat, spread = norm_parts(y_prev[at, :])
        back, d_gain, d_shift = norm_back(xhat, spread, gain, e)
        dprev[at, :] = back
        dprev_s.store(at)
        rounded = back.astype(bf16)
        dout1[at, :] = rounded
        gain_sum += d_gain
        shift_sum += d_shift
        out_sum += jnp.sum(rounded.astype(f32), axis=0, keepdims=True)
    do1_s.store()
    ctx1 = ctx1_s.wait()
    so_t.near[...] = dg(ctx1[hw : 2 * hw, :], dout1[...], 1, 0).astype(bf16)
    so_t.store()
    out_rows(g, ins[5].near, dout)
    put = slice(4 * hw, 5 * hw)
    g.near[put, :] = dg(ctx1[0:hw, :], dout1[...], 1, 0).astype(bf16)
    g.store(put)
    src_k = [k_m.wait(), k_t.wait()]
    weight_rows(g, grads, [halves_of([src_s]), src_k, src_k])
    q_sum, v_sum = position_sums(grads[0], grads[2])
    for short, ns in ((short_m, ns_m), (short_t, ns_t)):
        ns.near[...] = short[...]
        ns.near[S_GAIN : S_GAIN + 1, :] = gain_sum
        ns.near[S_SHIFT : S_SHIFT + 1, :] = shift_sum
        ns.near[S_SELF_OB : S_SELF_OB + 1, :] = out_sum
    ns_m.near[S_CROSS_B : S_CROSS_B + 1, :] = jnp.concatenate([q_sum, v_sum], axis=1)
    ns_m.store()
    ns_t.store()


def self_backward(core, ins, smalls, outs, _, scratch):
    do_s, x_m, x_t = ins[0:3]
    (short,) = smalls
    g = outs[0]
    grads = heads_backward(ins[3:8], outs[1:4], scratch[0], do_s.wait())
    src = [x_m.wait(), x_t.wait()]
    weight_rows(g, grads, [src] * 3)
    q_sum, v_sum = position_sums(grads[0], grads[2])
    own = jnp.concatenate([q_sum, v_sum], axis=1)
    index = lax.broadcasted_iota(jnp.int32, short.shape, 0)
    rows = jnp.where(index == S_SELF_B, jnp.broadcast_to(own, short.shape), short[...])
    start = 3 * grads[0].shape[0]
    stop, end = start + short.shape[0], g.near.shape[0]
    g.near[start:stop, :] = rows.astype(bf16)
    if stop < end:
        g.near[stop:end, :] = jnp.zeros((end - stop, g.near.shape[1]), bf16)
    g.store(slice(start, end))


def memory_gradient(core, ins, smalls, outs, _, scratch):
    out_m, out_t = outs
    sides = [[one.wait() for one in ins[0:3]], [one.wait() for one in ins[3:6]]]
    half = out_m.near.shape[0]
    for piece, out in ((1, out_t), (0, out_m)):
        at = slice(piece * half, (piece + 1) * half)
        total = None
        for dk, dv, w in sides:
            part = dg(dk[:, at], w[1], 0, 1) + dg(dv[:, at], w[2], 0, 1)
            total = part if total is None else total + part
        out.near[...] = total.astype(bf16)
        out.store()


def input_gradient(core, ins, smalls, outs, _, scratch):
    dy_s = ins[-1]
    out_m, out_t = outs
    sides = [[one.wait() for one in ins[0:4]], [one.wait() for one in ins[4:8]]]
    dy = dy_s.wait()
    half = out_m.near.shape[0]
    for piece, out in ((1, out_t), (0, out_m)):
        at = slice(piece * half, (piece + 1) * half)
        total = dy[at, :]
        for grads in sides:
            for j in range(3):
                total = total + dg(grads[j][:, at], grads[3][j], 0, 1)
        out.near[...] = total.astype(bf16)
        out.store()


def place_of(slot, core, length):
    place = slot[pl.ds(core, 1), :]
    half = length // 2
    return jnp.where(core == 0, place, jnp.where(place >= half, place - half, place + half))


def slot_matrix(slot, core, length):
    row = place_of(slot, core, length)
    shape = (length, row.shape[1])
    return jnp.where(lax.broadcasted_iota(jnp.int32, shape, 0) == jnp.broadcast_to(row, shape), 1.0, 0.0).astype(bf16)


def feed_forward(core, ins, smalls, outs, _, scratch):
    gs_m, gs_t, ws_m, ws_t, go_m, go_t, h2_s, wi_m, wi_t, wo_m, wo_t, y2_s = ins
    bi_m, bi_t, ob, gains, shifts, slot = smalls
    out_m, out_t, dy2_s, dc_s, g_m, g_t, small_m, small_t = outs
    onehot, tl, tr, e3, hid, dpre, slope, df_all, states = scratch
    length, width = h2_s.near.shape
    half = length // 2
    fw = wi_m.near.shape[1]
    sw = ws_m.near.shape[1]
    onehot[...] = slot_matrix(slot, core, length)
    for side, (gs, ws) in enumerate(((gs_m, ws_m), (gs_t, ws_t))):
        cols = slice(side * sw, (side + 1) * sw)
        left = dg(onehot[...], gs.wait()[...], 1, 0)
        tl[:, cols] = left.astype(bf16)
        tr[:, cols] = pltpu.roll(left, 1, 0).astype(bf16)
    ws = [ws_m.wait(), ws_t.wait()]
    go = [go_m.wait(), go_t.wait()]
    for i in range(length // TB):
        at = slice(i * TB, (i + 1) * TB)
        piece, inner = divmod(i * TB, half)
        total = go[piece][inner : inner + TB, :].astype(f32)
        for side in range(2):
            cols = slice(side * sw, (side + 1) * sw)
            total = total + dg(tl[at, cols], ws[side][0:width, :], 1, 1) + dg(tr[at, cols], ws[side][width : 2 * width, :], 1, 1)
        e3[at, :] = total
    h2, y2 = h2_s.wait(), y2_s.wait()
    wi = [wi_m.wait(), wi_t.wait()]
    wo = [wo_m.wait(), wo_t.wait()]
    dy2 = dy2_s.near
    dc = dc_s.near
    bias_in = [row_of(bi_m), row_of(bi_t)]
    bias_out = row_of(ob)
    gain2 = gains[1:2, :].astype(f32)
    gain3 = gains[2:3, :].astype(f32)
    shift3 = shifts[2:3, :].astype(f32)

    def one_block(i, sums):
        gain3_sum, shift3_sum, gain2_sum, shift2_sum, ffn_out_sum, cross_out_sum, in_m_sum, in_t_sum = sums
        at = pl.ds(pl.multiple_of(i * FFN_TB, FFN_TB), FFN_TB)
        hb = h2[at, :]
        y3 = hb.astype(f32) + bias_out
        for side in range(2):
            cols = slice(side * fw, (side + 1) * fw)
            pre = dg(hb, wi[side][...], 1, 0) + bias_in[side]
            square = pre * pre
            tanh = jnp.tanh(pre * (GELU_C + GELU_C * GELU_A * square))
            gate = 0.5 + 0.5 * tanh
            hidden = (pre * gate).astype(bf16)
            hid[at, cols] = hidden
            slope[:, cols] = gate + (0.5 * pre) * (1.0 - tanh * tanh) * (GELU_C + 3.0 * GELU_C * GELU_A * square)
            y3 = y3 + dg(hidden, wo[side][...], 1, 0)
        xhat, spread = norm_parts(y3)
        states[at, :] = (xhat * gain3 + shift3).astype(bf16)
        dy3, d_gain, d_shift = norm_back(xhat, spread, gain3, e3[at, :])
        gain3_sum += d_gain
        shift3_sum += d_shift
        df = dy3.astype(bf16)
        df_all[at, :] = df
        ffn_out_sum += jnp.sum(df.astype(f32), axis=0, keepdims=True)
        e2 = dy3
        in_sums = []
        for side, in_sum in enumerate((in_m_sum, in_t_sum)):
            cols = slice(side * fw, (side + 1) * fw)
            back = (dg(df, wo[side][...], 1, 1) * slope[:, cols]).astype(bf16)
            dpre[at, cols] = back
            in_sums.append(in_sum + jnp.sum(back.astype(f32), axis=0, keepdims=True))
            e2 = e2 + dg(back, wi[side][...], 1, 1)
        xhat, spread = norm_parts(y2[at, :])
        back2, d_gain, d_shift = norm_back(xhat, spread, gain2, e2)
        dy2[at, :] = back2
        rounded = back2.astype(bf16)
        dc[at, :] = rounded
        gain2_sum += d_gain
        shift2_sum += d_shift
        cross_out_sum += jnp.sum(rounded.astype(f32), axis=0, keepdims=True)
        return gain3_sum, shift3_sum, gain2_sum, shift2_sum, ffn_out_sum, cross_out_sum, in_sums[0], in_sums[1]

    row = jnp.zeros((1, width), f32)
    wide = jnp.zeros((1, fw), f32)
    sums = lax.fori_loop(0, length // FFN_TB, one_block, (row, row, row, row, row, row, wide, wide))
    dc_s.store()
    dy2_s.store()
    for piece, out in ((1, out_t), (0, out_m)):
        out.near[...] = states[piece * half : (piece + 1) * half, :]
        out.store()
    for side, g in ((1, g_t), (0, g_m)):
        for i in range(fw // width):
            block = slice(side * fw + i * width, side * fw + (i + 1) * width)
            rows = slice(width + i * width, 2 * width + i * width)
            g.near[rows, :] = dg(h2[...], dpre[:, block], 0, 0).astype(bf16)
            g.store(rows)
            rows = slice(width + fw + i * width, 2 * width + fw + i * width)
            g.near[rows, :] = dg(hid[:, block], df_all[...], 0, 0).astype(bf16)
            g.store(rows)
        cols = slice(side * sw, (side + 1) * sw)
        rows = slice(0, width)
        g.near[rows, 0:sw] = dg(states[...], tl[:, cols], 0, 0).astype(bf16)
        g.near[rows, sw : 2 * sw] = dg(states[...], tr[:, cols], 0, 0).astype(bf16)
        g.store(rows)
    for short, total, gs in ((small_m, sums[6], gs_m), (small_t, sums[7], gs_t)):
        short.near[...] = jnp.zeros(short.near.shape, f32)
        for at, one in ((S_GAIN + 2, 0), (S_SHIFT + 2, 1), (S_GAIN + 1, 2), (S_SHIFT + 1, 3), (S_FFN_OB, 4), (S_CROSS_OB, 5)):
            short.near[at : at + 1, :] = sums[one]
        for i in range(fw // width):
            short.near[S_FFN_B + i : S_FFN_B + i + 1, :] = total[:, i * width : (i + 1) * width]
        short.near[S_SLOT_B : S_SLOT_B + 1, 0:sw] = jnp.sum(gs.near[...].astype(f32), axis=0, keepdims=True)
        short.store()


def slot_forward(core, ins, smalls, outs, _, scratch):
    out_m, out_t, ws_m, ws_t = ins
    bs_m, bs_t, slot = smalls
    onehot, states = scratch
    length, width = states.shape
    half = length // 2
    onehot[...] = slot_matrix(slot, core, length)
    states[0:half, :] = out_m.wait()[...]
    states[half:length, :] = out_t.wait()[...]
    for ws_s, short, out in ((ws_t, bs_t, outs[1]), (ws_m, bs_m, outs[0])):
        ws = ws_s.wait()
        top = dg(states[...], ws[0:width, :], 1, 0)
        low = dg(states[...], ws[width : 2 * width, :], 1, 0)
        total = (top + pltpu.roll(low, length - 1, 0) + row_of(short)).astype(bf16)
        out.near[...] = dg(onehot[...], total, 0, 0).astype(bf16)
        out.store()


def joined(scalars, ins):
    bit = scalars[1]
    own, got = ins[0].wait(), ins[1].wait()
    return jnp.where(bit == 0, own[...], got[...]), jnp.where(bit == 0, got[...], own[...])


def put_qkv(out, buf, hw):
    for j in range(3):
        out.near[j, 0:hw, :] = buf[j * hw : (j + 1) * hw, 0:hw].astype(f32)
        out.near[j, hw : 2 * hw, :] = buf[j * hw : (j + 1) * hw, hw : 2 * hw].astype(f32)
    out.store()


def unpack_cross(scalars, ins, smalls, outs, small_outs, scratch):
    (buf,) = scratch
    count = buf.shape[0] // 2
    buf[0:count, :], buf[count:, :] = joined(scalars, ins)
    qkv, cross_out, self_out = outs
    hw = cross_out.near.shape[0]
    put_qkv(qkv, buf, hw)
    cross_out.near[...] = buf[3 * hw : 4 * hw, :].astype(f32)
    cross_out.store()
    self_out.near[...] = buf[4 * hw : 5 * hw, :].astype(f32)
    self_out.store()


def unpack_self(scalars, ins, smalls, outs, small_outs, scratch):
    (buf,) = scratch
    count = buf.shape[0] // 2
    buf[0:count, :], buf[count:, :] = joined(scalars, ins)
    (qkv,) = outs
    hw = qkv.near.shape[2]
    put_qkv(qkv, buf, hw)
    self_b, self_ob, cross_b, cross_ob, ffn_b, ffn_ob, gains, shifts, slot_b = small_outs
    short = buf[3 * hw : 3 * hw + 16, :].astype(f32)
    width = short.shape[1]
    for ref, at in ((self_b, S_SELF_B), (cross_b, S_CROSS_B)):
        ref[0:1, :] = short[at : at + 1, 0:hw]
        ref[1:2, :] = short[at : at + 1, hw : 2 * hw]
    for ref, at in ((self_ob, S_SELF_OB), (cross_ob, S_CROSS_OB), (ffn_ob, S_FFN_OB)):
        ref[...] = short[at : at + 1, :].reshape(width)
    wide = ffn_b.shape[0] // width
    ffn_b[...] = jnp.concatenate([short[S_FFN_B + i : S_FFN_B + i + 1, :] for i in range(wide)], axis=1).reshape(wide * width)
    gains[...] = short[S_GAIN : S_GAIN + 3, :]
    shifts[...] = short[S_SHIFT : S_SHIFT + 3, :]
    slot_b[...] = short[S_SLOT_B : S_SLOT_B + 1, 0 : slot_b.shape[0]].reshape(slot_b.shape[0])


def unpack_ffn(scalars, ins, smalls, outs, _, scratch):
    (buf,) = scratch
    count = buf.shape[0] // 2
    buf[0:count, :], buf[count:, :] = joined(scalars, ins)
    slot_w, ffn_in, ffn_out = outs
    width = buf.shape[1]
    sw = slot_w.near.shape[1]
    slot_w.near[0:width, :] = buf[0:width, 0:sw].astype(f32)
    slot_w.near[width:, :] = buf[0:width, sw : 2 * sw].astype(f32)
    slot_w.store()
    fw = ffn_in.near.shape[1]
    for i in range(fw // width):
        ffn_in.near[:, i * width : (i + 1) * width] = buf[(i + 1) * width : (i + 2) * width, :].astype(f32)
    ffn_in.store()
    ffn_out.near[...] = buf[width + fw :, :].astype(f32)
    ffn_out.store()


def swap(x):
    return lax.ppermute(x, "tensor", [(0, 1), (1, 0)])


class RowSum:
    def __init__(self, x, dp_size, dp_index, core):
        bits = dp_size.bit_length() - 1
        orders = [list(range(bits)), list(range(bits))]
        if bits > 2:
            orders[1] = [1, 2, 0] + list(range(3, bits))
        self.plan = []
        for step in range(bits):
            pairs = []
            for device in range(dp_size):
                for c in range(2):
                    pairs.append((device * 2 + c, (device ^ (1 << orders[c][step])) * 2 + c))
            bit = jnp.where(core == 0, (dp_index >> orders[0][step]) & 1, (dp_index >> orders[1][step]) & 1)
            self.plan.append((pairs, bit.astype(jnp.int32)))
        self.x = x
        self.step = 0
        self.done = False
        self.cut()

    def cut(self):
        if self.step >= len(self.plan) - 1:
            self.away = self.kept = self.x
            return
        bit = self.plan[self.step][1]
        count = self.x.shape[0] // 2
        self.away = lax.dynamic_slice_in_dim(self.x, (1 - bit) * count, count, 0)
        self.kept = lax.dynamic_slice_in_dim(self.x, bit * count, count, 0)

    def scatter(self, *beside):
        got = lax.ppermute(self.away, ("dp", "tensor"), self.plan[self.step][0])
        if beside:
            got = lax.optimization_barrier((got, *beside))[0]
        self.x = (self.kept.astype(f32) + got.astype(f32)).astype(bf16)
        self.step += 1
        self.done = self.step == len(self.plan)
        self.cut()
        if self.done:
            self.step -= 1

    def gather(self, last):
        while self.step > last:
            pairs, bit = self.plan[self.step - 1]
            got = lax.ppermute(self.x, ("dp", "tensor"), pairs)
            self.step -= 1
            if self.step == 0:
                return self.x, got
            first = lax.broadcasted_iota(jnp.int32, (2,) + self.x.shape, 0) == bit
            self.x = jnp.where(first, self.x[None], got[None]).reshape((2 * self.x.shape[0],) + self.x.shape[1:])


def shards(dp_size, *args):
    (tokens, memory, dec_segment, enc_segment, slot_left, self_qkv, self_bias, self_out, self_out_bias,
     cross_qkv, cross_bias, cross_out, cross_out_bias, ffn_in, ffn_in_bias, ffn_out, ffn_out_bias,
     norm_gain, norm_bias, slot_weight, slot_bias, grad_output, grad_slots) = args
    core_index = lax.axis_index("tensor")
    dp_index = lax.axis_index("dp")
    core = core_index.astype(jnp.int32).reshape(1)
    half, width = tokens.shape[1], tokens.shape[2]
    length = 2 * half
    hw = self_qkv.shape[2]
    heads = 2 * hw // HEAD_DIM
    fw = ffn_in.shape[1]
    wide = fw // width
    sw = slot_weight.shape[1]
    slots = slot_left.shape[1]

    tokens_t = swap(tokens)
    self_qkv_t = swap(self_qkv)
    self_bias_t = swap(self_bias)
    self_out_t = swap(self_out)
    memory_t = swap(memory)
    cross_qkv_t = swap(cross_qkv)
    cross_bias_t = swap(cross_bias)
    cross_out_t = swap(cross_out)
    grad_slots_t = swap(grad_slots)
    slot_weight_t = swap(slot_weight)
    grad_output_t = swap(grad_output)
    ffn_in_t = swap(ffn_in)
    ffn_in_bias_t = swap(ffn_in_bias)
    ffn_out_t = swap(ffn_out)
    slot_bias_t = swap(slot_bias)

    aug = (heads, AUG, length)
    blocks = length // TB
    forward_outs = [(aug, bf16, 1), (aug, bf16, 1), (aug, bf16, 1), ((2 * hw, length), bf16, 1),
                    ((length, width), f32, blocks), ((length, width), bf16, blocks)]
    qa, ka, va, ctx, y1, h1 = staged_call(
        functools.partial(attend_forward, False), core,
        [(tokens, "core"), (tokens_t, "core"), (self_qkv, None), (self_qkv_t, None), (self_out, None), (self_out_t, None)],
        [self_bias, self_bias_t, self_out_bias, norm_gain, norm_bias, dec_segment], forward_outs, micros=18)
    qa2, ka2, va2, ctx2, y2, h2 = staged_call(
        functools.partial(attend_forward, True), core,
        [(h1, None), (memory, "core"), (memory_t, "core"), (cross_qkv, None), (cross_qkv_t, None), (cross_out, None),
         (cross_out_t, None)],
        [cross_bias, cross_bias_t, cross_out_bias, norm_gain, norm_bias, dec_segment, enc_segment], forward_outs, micros=18)
    g1_rows = width + 2 * fw
    half_out = ((half, width), bf16, 1)
    out_m, out_t, dy2, dc, g1_m, g1_t, short1_m, short1_t = staged_call(
        feed_forward, core,
        [(grad_slots, "core"), (grad_slots_t, "core"), (slot_weight, None), (slot_weight_t, None), (grad_output, "core"),
         (grad_output_t, "core"), (h2, None), (ffn_in, None), (ffn_in_t, None), (ffn_out, None), (ffn_out_t, None),
         (y2, None)],
        [ffn_in_bias, ffn_in_bias_t, ffn_out_bias, norm_gain, norm_bias, slot_left],
        [half_out, half_out, ((length, width), f32, 1), ((length, width), bf16, 1), ((g1_rows, width), bf16, 1 + 2 * wide),
         ((g1_rows, width), bf16, 1 + 2 * wide), ((16, width), f32, 1), ((16, width), f32, 1)],
        scratch=[pltpu.VMEM((length, slots), bf16), pltpu.VMEM((length, 2 * sw), bf16), pltpu.VMEM((length, 2 * sw), bf16),
                 pltpu.VMEM((length, width), f32), pltpu.VMEM((length, 2 * fw), bf16), pltpu.VMEM((length, 2 * fw), bf16),
                 pltpu.VMEM((FFN_TB, 2 * fw), f32), pltpu.VMEM((length, width), bf16), pltpu.VMEM((length, width), bf16)],
        after=[slot_bias_t], micros=25)
    st_m, st_t = staged_call(
        slot_forward, core, [(out_m, None), (out_t, None), (slot_weight, None), (slot_weight_t, None)],
        [slot_bias, slot_bias_t, slot_left], [((slots, sw), bf16, 1), ((slots, sw), bf16, 1)],
        scratch=[pltpu.VMEM((length, slots), bf16), pltpu.VMEM((length, width), bf16)], micros=4)
    g1_got = lax.optimization_barrier((swap(g1_t), st_m))[0]
    g1 = (g1_m.astype(f32) + g1_got.astype(f32)).astype(bf16)

    def packed(total):
        return total.reshape(dp_size, total.shape[0] // dp_size, width)

    def added(kept, got):
        return (kept.astype(f32) + got.astype(f32)).astype(bf16)

    sum1 = RowSum(packed(g1), dp_size, dp_index, core_index)
    count = heads // 2
    grad_out = ((hw, length), bf16, 1)
    wide_f32 = ((length, width), f32, blocks)
    short_out = ((16, width), f32, 1)
    da_scratch = [pltpu.VMEM((count, AUG, length), bf16)]

    def head_inputs(side, wo, c, v, q, k):
        of = slice(side * count, (side + 1) * count)
        return [(wo[side], None), (c, slice(side * hw, (side + 1) * hw)), (v, of), (q, of), (k, of)]

    cross_inputs = [(dc, None), (h1, None), (memory, "core"), (memory_t, "core")]
    cross_wo = (cross_out, cross_out_t)
    g2_t, short_t, *cross_t = staged_call(
        cross_backward_first, core, cross_inputs + head_inputs(1, cross_wo, ctx2, va2, qa2, ka2), [short1_t],
        [((4 * hw, width), bf16, 4), short_out] + [grad_out] * 3, scratch=da_scratch, after=[sum1.away], micros=15)
    sum1.scatter()
    g2_m, short2_m, short2_t, *cross_m, dy1, do1, so_t = staged_call(
        cross_backward_second, core,
        cross_inputs + head_inputs(0, cross_wo, ctx2, va2, qa2, ka2)
        + [(dy2, None), (y1, None), (cross_t[0], None), (cross_qkv, slice(0, 1)), (cross_qkv_t, slice(0, 1)), (ctx, None)],
        [norm_gain, short1_m, short_t],
        [((5 * hw, width), bf16, 5), short_out, short_out] + [grad_out] * 3
        + [wide_f32, ((length, width), bf16, 1), ((hw, width), bf16, 1)],
        scratch=da_scratch, after=[sum1.away], micros=17)
    sum1.scatter()
    dmem_m, dmem_t = staged_call(
        memory_gradient, core,
        [(cross_m[1], None), (cross_m[2], None), (cross_qkv, None), (cross_t[1], None), (cross_t[2], None), (cross_qkv_t, None)],
        [], [half_out, half_out], after=[sum1.away], micros=4)
    so_got = lax.optimization_barrier((swap(so_t), dmem_m))[0]
    sum2 = RowSum(packed(added(g2_m, jnp.concatenate([swap(g2_t), so_got], axis=0))), dp_size, dp_index, core_index)
    sum1.scatter()
    g3_rows = 3 * hw + 16 + (-(3 * hw + 16)) % 128
    g3_rows += -g3_rows % dp_size
    sides = {}
    held = [dmem_m]
    for side in (1, 0):
        g3, *grads = staged_call(
            self_backward, core,
            [(do1, None), (tokens, "core"), (tokens_t, "core")] + head_inputs(side, (self_out, self_out_t), ctx, va, qa, ka),
            [(short2_m, short2_t)[side]], [((g3_rows, width), bf16, 4)] + [grad_out] * 3, scratch=da_scratch,
            after=held + [sum1.away, sum2.away], micros=15)
        if not sum1.done:
            sum1.scatter()
        sum2.scatter()
        held = []
        sides[side] = (g3, [(g, None) for g in grads] + [((self_qkv, self_qkv_t)[side], None)])
    while not sum1.done:
        sum1.scatter()
    sum1.gather(len(sum1.plan) - 2)

    def together(kept, sent):
        got = swap(sent)
        return jnp.where(lax.broadcasted_iota(jnp.int32, (2,) + kept.shape, 0) == core_index, kept[None], got[None])

    output = together(out_m, out_t)
    slot_states = together(st_m, st_t)
    grad_memory = together(dmem_m, dmem_t)
    g3_got = lax.optimization_barrier((swap(sides[1][0]), sum1.x, sum2.away))[0]
    sum3 = RowSum(packed(added(sides[0][0], g3_got)), dp_size, dp_index, core_index)
    dx_m, dx_t = staged_call(input_gradient, core, sides[0][1] + sides[1][1] + [(dy1, None)], [], [half_out, half_out], micros=5)
    sum3.scatter(output, slot_states, grad_memory)
    while not sum2.done:
        sum2.scatter()
    while not sum3.done:
        sum3.scatter()
    grad_input = together(dx_m, dx_t)

    def ends(total):
        own, got = total.gather(0)
        flat = lambda x: x.reshape(-1, width)
        return jnp.stack([core_index.astype(jnp.int32), total.plan[0][1]]), [(flat(own), None), (flat(got), None)]

    qkv_out = ((3, 2 * hw, hw), f32, 1)
    scalars, halves = ends(sum1)
    grad_slot_weight, grad_ffn_in, grad_ffn_out = staged_call(
        unpack_ffn, scalars, halves, [], [((2 * width, sw), f32, 1), ((width, fw), f32, 1), ((fw, width), f32, 1)],
        scratch=[pltpu.VMEM((g1_rows, width), bf16)], micros=4)
    scalars, halves = ends(sum2)
    grad_cross_qkv, grad_cross_out, grad_self_out = staged_call(
        unpack_cross, scalars, halves, [], [qkv_out, ((hw, width), f32, 1), ((hw, width), f32, 1)],
        scratch=[pltpu.VMEM((5 * hw, width), bf16)], micros=3)
    scalars, halves = ends(sum3)
    (grad_self_qkv, grad_self_bias, grad_self_out_bias, grad_cross_bias, grad_cross_out_bias, grad_ffn_in_bias,
     grad_ffn_out_bias, grad_norm_gain, grad_norm_bias, grad_slot_bias) = staged_call(
        unpack_self, scalars, halves, [], [qkv_out],
        [((2, hw), f32), ((width,), f32), ((2, hw), f32), ((width,), f32), ((fw,), f32), ((width,), f32), ((3, width), f32),
         ((3, width), f32), ((sw,), f32)],
        scratch=[pltpu.VMEM((g3_rows, width), bf16)], micros=3)
    return (
        output, slot_states, grad_input, grad_memory, grad_self_qkv, grad_self_bias, grad_self_out, grad_self_out_bias,
        grad_cross_qkv, grad_cross_bias, grad_cross_out, grad_cross_out_bias, grad_ffn_in, grad_ffn_in_bias, grad_ffn_out,
        grad_ffn_out_bias, grad_norm_gain, grad_norm_bias, grad_slot_weight, grad_slot_bias,
    )


def solution(mesh):
    row3 = P("dp", "tensor", None)
    seg = P("dp", None)
    col3 = P(None, None, "tensor")
    col2 = P(None, "tensor")
    out2 = P("tensor", None)
    one = P("tensor")
    in_specs = (row3, row3, seg, seg, seg, col3, col2, out2, P(), col3, col2, out2, P(), col2, one, out2, P(), P(), P(),
                col2, one, row3, P("dp", None, "tensor"))
    out_specs = (row3, P("dp", None, "tensor"), row3, row3, col3, col2, out2, P(), col3, col2, out2, P(), col2, one, out2,
                 P(), P(), P(), col2, one)
    body = functools.partial(shards, mesh.shape["dp"])
    return jax.shard_map(body, mesh=mesh, in_specs=in_specs, out_specs=out_specs, check_vma=False)
```

profile of v0, /device:TPU:0, one launch (start us, length us, event | category | flops | bytes accessed | tf_op | source)
XLA Modules:
  0.0 252.9 jit_solution(10942428879847552267)
XLA Ops:
  2.2 3.0 %collective-permute-done.14.refs_19_.refs_6_ = bf16[256]{0:T(256)(128)(2,1)S(1)} collective-permute-done((bf16[256]{0:T(256)(128)(2,1)}, bf16[256]{0:T(256)(128)(2,1)S(1)}, u32[]{:S(2)}, u32[]{:S(2)}) %collective-permute-start.14) | collective-permute-done | bytes 544 | tf_op jit(solution)/shard_map/ppermute | solution.py:652
  7.3 17.8 %shard_map.374 = (bf16[8,80,1024]{2,1,0:T(8,128)(2,1)}, bf16[8,80,1024]{2,1,0:T(8,128)(2,1)}, bf16[8,80,1024]{2,1,0:T(8,128)(2,1)}, bf16[512,1024]{1,0:T(8,128)(...) custom-call(s32[1]{0:T(128)} %bitcast.refs_0_, bf16[2,512,512]{2,1,0:T(8,128)(2,1)} %refs_2_.5, ...), custom_call_target="tpu_custom_call" | custom-call | flops 19800000512 | bytes 1024 | tf_op jit(solution)/shard_map/pallas_call | solution.py:131
  27.5 27.8 %shard_map.375 = (bf16[8,80,1024]{2,1,0:T(8,128)(2,1)}, bf16[8,80,1024]{2,1,0:T(8,128)(2,1)}, bf16[8,80,1024]{2,1,0:T(8,128)(2,1)}, bf16[512,1024]{1,0:T(8,128)(...) custom-call(s32[1]{0:T(128)} %bitcast.refs_0_, bf16[1024,512]{1,0:T(8,128)(2,1)} %get-tuple-element.87.refs_1_.refs_2_, ...), custom_call_target="tpu_custom_call" | custom-call | flops 19800000512 | bytes 1024 | tf_op jit(solution)/shard_map/pallas_call | solution.py:131
  57.3 24.7 %shard_map.376 = (bf16[512,512]{1,0:T(8,128)(2,1)}, bf16[512,512]{1,0:T(8,128)(2,1)}, f32[1024,512]{1,0:T(8,128)}, bf16[1024,512]{1,0:T(8,128)(2,1)}, bf16[2560,...) custom-call(s32[1]{0:T(128)} %bitcast.refs_0_, ...), custom_call_target="tpu_custom_call" | custom-call | flops 27499999232 | bytes 1024 | tf_op jit(solution)/shard_map/pallas_call | solution.py:131
  82.3 5.8 %shard_map.377 = (bf16[512,256]{1,0:T(8,128)(2,1)}, bf16[512,256]{1,0:T(8,128)(2,1)}) custom-call(s32[1]{0:T(128)} %bitcast.refs_0_, bf16[512,512]{1,0:T(8,128)(2,1)} %get-tuple-element.90.refs_1_, bf16[512,512]{1,0:T(8,128)(2,1)} %get-tuple-element.91.refs_2_, bf16[1024,256]{1,0:T(8,128)(2,1)} %refs_3_.8, bf16[1024,256]{1,0:T(8,128)(2,1)} %copy-done.19, ...), custom_call_target="tpu_custom_call" | custom-call | flops 4400000000 | bytes 1024 | tf_op jit(solution)/shard_map/pallas_call | solution.py:131
  91.8 2.5 add_convert_fusion
  94.4 2.8 %collective-permute-start.18 = (bf16[8,160,512]{2,1,0:T(8,128)(2,1)S(1)}, bf16[8,160,512]{2,1,0:T(8,128)(2,1)S(1)}, u32[]{:S(2)}, u32[]{:S(2)}) collective-permute-start(bf16[8,160,512]{2,1,0:T(8,128)(2,1)S(1)} %constant_dynamic-slice_fusion.8.refs_11_), channel_id=1, source_target_pairs={{0,2},{1,5},{2,0},{3,7},{4,6},{5,1},{6,4},{7,3},{8,10},{9,13},{10,... | collective-permute-start | bytes 3932168 | tf_op jit(solution)/shard_map/ppermute | solution.py:684
  97.2 16.4 %shard_map.378 = (bf16[1024,512]{1,0:T(8,128)(2,1)}, f32[16,512]{1,0:T(8,128)}, bf16[256,1024]{1,0:T(8,128)(2,1)}, bf16[256,1024]{1,0:T(8,128)(2,1)}, bf16[256,1024]{1,0:T(8,128)(2,1)}) custom-call(s32[1]{0:T(128)} %bitcast.refs_0_, bf16[1024,512]{1,0:T(8,128)(2,1)} %get-tuple-element.94.refs_1_, bf16[1024,512]{1,0:T(8,128)(2,1)} %get-tuple-element.87.refs_1_.refs_2_, ...), custom_call_target="tpu_custom_call" | custom-call | flops 16499999744 | bytes 1024 | tf_op jit(solution)/shard_map/pallas_call | solution.py:131
  115.7 18.8 %shard_map.379 = (bf16[1280,512]{1,0:T(8,128)(2,1)}, f32[16,512]{1,0:T(8,128)}, f32[16,512]{1,0:T(8,128)}, bf16[256,1024]{1,0:T(8,128)(2,1)}, bf16[256,1024]{1,0...) custom-call(s32[1]{0:T(128)} %bitcast.refs_0_, ...), custom_call_target="tpu_custom_call" | custom-call | flops 18699999232 | bytes 1024 | tf_op jit(solution)/shard_map/pallas_call | solution.py:131
  136.5 4.2 %shard_map.380 = (bf16[512,512]{1,0:T(8,128)(2,1)}, bf16[512,512]{1,0:T(8,128)(2,1)}) custom-call(s32[1]{0:T(128)} %bitcast.refs_0_, bf16[256,1024]{1,0:T(8,128)(2,1)} %get-tuple-element.117.refs_1_, bf16[256,1024]{1,0:T(8,128)(2,1)} %get-tuple-element.118.refs_2_, bf16[3,512,256]{2,1,0:T(8,128)(2,1)} %refs_3_.11, ...), custom_call_target="tpu_custom_call" | custom-call | flops 4400000000 | bytes 1024 | tf_op jit(solution)/shard_map/pallas_call | solution.py:131
  142.6 2.7 %collective-permute-start.21 = (bf16[2,160,512]{2,1,0:T(8,128)(2,1)S(1)}, bf16[2,160,512]{2,1,0:T(8,128)(2,1)S(1)}, u32[]{:S(2)}, u32[]{:S(2)}) collective-permute-start(bf16[2,160,512]{2,1,0:T(8,128)(2,1)S(1)} %add_convert_fusion.9.refs_11_), channel_id=1, source_target_pairs={{0,16},{1,17},{2,18},{3,19},{4,20},{5,21},{6,22},{7,23},{8,24},{9,... | collective-permute-start | bytes 983048 | tf_op jit(solution)/shard_map/ppermute | solution.py:684
  145.3 15.4 %shard_map.382 = (bf16[896,512]{1,0:T(8,128)(2,1)}, bf16[256,1024]{1,0:T(8,128)(2,1)}, bf16[256,1024]{1,0:T(8,128)(2,1)}, bf16[256,1024]{1,0:T(8,128)(2,1)}) custom-call(s32[1]{0:T(128)} %bitcast.refs_0_, bf16[1024,512]{1,0:T(8,128)(2,1)} %get-tuple-element.109.refs_1_, bf16[2,512,512]{2,1,0:T(8,128)(2,1)} %refs_2_.5, bf16[2,512,512]{2,1,0:T(8,128)(2,1)} %copy-done.9, ...), custom_call_target="tpu_custom_call" | custom-call | flops 16499999744 | bytes 1024 | tf_op jit(solution)/shard_map/pallas_call | solution.py:131
  162.9 15.4 %shard_map.381 = (bf16[896,512]{1,0:T(8,128)(2,1)}, bf16[256,1024]{1,0:T(8,128)(2,1)}, bf16[256,1024]{1,0:T(8,128)(2,1)}, bf16[256,1024]{1,0:T(8,128)(2,1)}) custom-call(s32[1]{0:T(128)} %bitcast.refs_0_, bf16[1024,512]{1,0:T(8,128)(2,1)} %get-tuple-element.109.refs_1_, bf16[2,512,512]{2,1,0:T(8,128)(2,1)} %refs_2_.5, bf16[2,512,512]{2,1,0:T(8,128)(2,1)} %copy-done.9, ...), custom_call_target="tpu_custom_call" | custom-call | flops 16499999744 | bytes 1024 | tf_op jit(solution)/shard_map/pallas_call | solution.py:131
  178.3 5.8 %shard_map.383 = (bf16[512,512]{1,0:T(8,128)(2,1)}, bf16[512,512]{1,0:T(8,128)(2,1)}) custom-call(s32[1]{0:T(128)} %bitcast.refs_0_, bf16[256,1024]{1,0:T(8,128)(2,1)} %get-tuple-element.123.refs_1_, bf16[256,1024]{1,0:T(8,128)(2,1)} %get-tuple-element.124.refs_2_, bf16[256,1024]{1,0:T(8,128)(2,1)} %get-tuple-element.125.refs_3_, ...), custom_call_target="tpu_custom_call" | custom-call | flops 5500000256 | bytes 1024 | tf_op jit(solution)/shard_map/pallas_call | solution.py:131
  187.3 4.2 %collective-permute-done.37 = bf16[2,80,512]{2,1,0:T(8,128)(2,1)S(1)} collective-permute-done((bf16[2,80,512]{2,1,0:T(8,128)(2,1)S(1)}, bf16[2,80,512]{2,1,0:T(8,128)(2,1)S(1)}, u32[]{:S(2)}, u32[]{:S(2)}) %collective-permute-start.37) | collective-permute-done | bytes 163872 | tf_op jit(solution)/shard_map/ppermute | solution.py:684
  194.8 5.2 %collective-permute-done.30 = bf16[8,56,512]{2,1,0:T(8,128)(2,1)S(1)} collective-permute-done((bf16[8,56,512]{2,1,0:T(8,128)(2,1)S(1)}, bf16[8,56,512]{2,1,0:T(8,128)(2,1)S(1)}, u32[]{:S(2)}, u32[]{:S(2)}) %collective-permute-start.30) | collective-permute-done | bytes 458784 | tf_op jit(solution)/shard_map/ppermute | solution.py:684
  202.6 3.6 %collective-permute-done.31 = bf16[4,56,512]{2,1,0:T(8,128)(2,1)S(1)} collective-permute-done((bf16[4,56,512]{2,1,0:T(8,128)(2,1)S(1)}, bf16[4,56,512]{2,1,0:T(8,128)(2,1)S(1)}, u32[]{:S(2)}, u32[]{:S(2)}) %collective-permute-start.31) | collective-permute-done | bytes 229408 | tf_op jit(solution)/shard_map/ppermute | solution.py:684
  214.2 5.4 %collective-permute-done.40 = bf16[4,80,512]{2,1,0:T(8,128)(2,1)S(1)} collective-permute-done((bf16[4,80,512]{2,1,0:T(8,128)(2,1)S(1)}, bf16[4,80,512]{2,1,0:T(8,128)(2,1)S(1)}, u32[]{:S(2)}, u32[]{:S(2)}) %collective-permute-start.40) | collective-permute-done | bytes 327712 | tf_op jit(solution)/shard_map/ppermute | solution.py:697
  220.6 1.9 collective-permute-start.41
  223.2 4.1 %collective-permute-done.34 = bf16[2,56,512]{2,1,0:T(8,128)(2,1)S(1)} collective-permute-done((bf16[2,56,512]{2,1,0:T(8,128)(2,1)S(1)}, bf16[2,56,512]{2,1,0:T(8,128)(2,1)S(1)}, u32[]{:S(2)}, u32[]{:S(2)}) %collective-permute-start.34) | collective-permute-done | bytes 114720 | tf_op jit(solution)/shard_map/ppermute | solution.py:697
  231.0 5.1 %collective-permute-done.35 = bf16[4,56,512]{2,1,0:T(8,128)(2,1)} collective-permute-done((bf16[4,56,512]{2,1,0:T(8,128)(2,1)S(1)}, bf16[4,56,512]{2,1,0:T(8,128)(2,1)}, u32[]{:S(2)}, u32[]{:S(2)}) %collective-permute-start.35) | collective-permute-done | bytes 229408 | tf_op jit(solution)/shard_map/ppermute | solution.py:697
  238.2 3.5 %shard_map.385 = (f32[3,512,256]{2,1,0:T(8,128)}, f32[256,512]{1,0:T(8,128)}, f32[256,512]{1,0:T(8,128)}) custom-call(s32[2]{0:T(128)S(1)} %pad_add_fusion.refs_0_, bf16[640,512]{1,0:T(8,128)(2,1)} %bitcast_select_fusion.3.refs_1_, bf16[640,512]{1,0:T(8,128)(2,1)} %bitcast.20.refs_2_), custom_call_target="tpu_custom_call" | custom-call | flops 3300000000 | bytes 1024 | tf_op jit(solution)/shard_map/pallas_call | solution.py:131
  243.5 4.7 %shard_map.386 = (f32[1024,256]{1,0:T(8,128)}, f32[512,1024]{1,0:T(8,128)}, f32[1024,512]{1,0:T(8,128)}) custom-call(s32[2]{0:T(128)S(1)} %pad_add_fusion.refs_0_, bf16[1280,512]{1,0:T(8,128)(2,1)} %bitcast_select_fusion.1.refs_1_, bf16[1280,512]{1,0:T(8,128)(2,1)} %bitcast.25.refs_2_), custom_call_target="tpu_custom_call" | custom-call | flops 4400000000 | bytes 1024 | tf_op jit(solution)/shard_map/pallas_call | solution.py:131
  249.0 3.6 %shard_map.384 = (f32[3,512,256]{2,1,0:T(8,128)}, f32[2,256]{1,0:T(2,128)}, f32[512]{0:T(512)}, f32[2,256]{1,0:T(2,128)}, f32[512]{0:T(512)}, /*index=5*/f32[102...) custom-call(s32[2]{0:T(128)S(1)} %pad_add_fusion.refs_0_, ...), custom_call_target="tpu_custom_call" | custom-call | flops 3300000000 | bytes 1024 | tf_op jit(solution)/shard_map/pallas_call | solution.py:131
  (182 shorter events, 47.2 us)
Async XLA Ops:
  5.2 21.3 %collective-permute-start.7 = (bf16[2,512,512]{2,1,0:T(8,128)(2,1)}, bf16[2,512,512]{2,1,0:T(8,128)(2,1)S(1)}, u32[]{:S(2)}, u32[]{:S(2)}) collective-permute-start(bf16[2,512,512]{2,1,0:T(8,128)(2,1)} %refs_3_.10), channel_id=1, source_target_pairs={{0,1},{1,0},{2,3},{3,2},{4,5},{5,4},{6,7},{7,6},{8,9},{9,8},{10,11... | collective-permute-start | bytes 3145736 | tf_op jit(solution)/shard_map/ppermute | solution.py:652
  5.6 20.6 %collective-permute-start.8 = (bf16[3,512,256]{2,1,0:T(8,128)(2,1)}, bf16[3,512,256]{2,1,0:T(8,128)(2,1)S(1)}, u32[]{:S(2)}, u32[]{:S(2)}) collective-permute-start(bf16[3,512,256]{2,1,0:T(8,128)(2,1)} %refs_3_.11), channel_id=1, source_target_pairs={{0,1},{1,0},{2,3},{3,2},{4,5},{5,4},{6,7},{7,6},{8,9},{9,8},{10,11... | collective-permute-start | bytes 2359304 | tf_op jit(solution)/shard_map/ppermute | solution.py:652
  5.7 20.2 %collective-permute-start.9 = (bf16[256,512]{1,0:T(8,128)(2,1)}, bf16[256,512]{1,0:T(8,128)(2,1)S(1)}, u32[]{:S(2)}, u32[]{:S(2)}) collective-permute-start(bf16[256,512]{1,0:T(8,128)(2,1)} %refs_5_.7), channel_id=1, source_target_pairs={{0,1},{1,0},{2,3},{3,2},{4,5},{5,4},{6,7},{7,6},{8,9},{9,8},{10,11... | collective-permute-start | bytes 786440 | tf_op jit(solution)/shard_map/ppermute | solution.py:652
  6.1 19.1 %collective-permute-start.10 = (bf16[2,256]{1,0:T(2,128)(2,1)}, bf16[2,256]{1,0:T(2,128)(2,1)S(1)}, u32[]{:S(2)}, u32[]{:S(2)}) collective-permute-start(bf16[2,256]{1,0:T(2,128)(2,1)} %refs_8_.2), channel_id=1, source_target_pairs={{0,1},{1,0},{2,3},{3,2},{4,5},{5,4},{6,7},{7,6},{8,9},{9,8},{10,11... | collective-permute-start | bytes 3080 | tf_op jit(solution)/shard_map/ppermute | solution.py:652
  6.2 19.3 %collective-permute-start.13 = (bf16[1024]{0:T(1024)(128)(2,1)}, bf16[1024]{0:T(1024)(128)(2,1)S(1)}, u32[]{:S(2)}, u32[]{:S(2)}) collective-permute-start(bf16[1024]{0:T(1024)(128)(2,1)} %refs_13_.4), channel_id=1, source_target_pairs={{0,1},{1,0},{2,3},{3,2},{4,5},{5,4},{6,7},{7,6},{8,9},{9,8},{10,11... | collective-permute-start | bytes 6152 | tf_op jit(solution)/shard_map/ppermute | solution.py:652
  25.2 30.1 %collective-permute-start = (bf16[2,512,256]{2,1,0:T(8,128)(2,1)S(1)}, bf16[2,512,256]{2,1,0:T(8,128)(2,1)S(1)}, u32[]{:S(2)}, u32[]{:S(2)}) collective-permute-start(bf16[2,512,256]{2,1,0:T(8,128)(2,1)S(1)} %copy-done.16), channel_id=1, source_target_pairs={{0,1},{1,0},{2,3},{3,2},{4,5},{5,4},{6,7},{7,6},{8,9},{9,8},{10,11... | collective-permute-start | bytes 1572872 | tf_op jit(solution)/shard_map/ppermute | solution.py:652
  25.6 29.8 %collective-permute-start.1 = (bf16[1024,256]{1,0:T(8,128)(2,1)S(1)}, bf16[1024,256]{1,0:T(8,128)(2,1)S(1)}, u32[]{:S(2)}, u32[]{:S(2)}) collective-permute-start(bf16[1024,256]{1,0:T(8,128)(2,1)S(1)} %copy-done.17), channel_id=1, source_target_pairs={{0,1},{1,0},{2,3},{3,2},{4,5},{5,4},{6,7},{7,6},{8,9},{9,8},{10,11... | collective-permute-start | bytes 1572872 | tf_op jit(solution)/shard_map/ppermute | solution.py:652
  25.9 29.5 %collective-permute-start.2 = (bf16[2,512,512]{2,1,0:T(8,128)(2,1)S(1)}, bf16[2,512,512]{2,1,0:T(8,128)(2,1)S(1)}, u32[]{:S(2)}, u32[]{:S(2)}) collective-permute-start(bf16[2,512,512]{2,1,0:T(8,128)(2,1)S(1)} %copy-done.6), channel_id=1, source_target_pairs={{0,1},{1,0},{2,3},{3,2},{4,5},{5,4},{6,7},{7,6},{8,9},{9,8},{10,11... | collective-permute-start | bytes 3145736 | tf_op jit(solution)/shard_map/ppermute | solution.py:652
  26.2 29.2 %collective-permute-start.11 = (bf16[512,1024]{1,0:T(8,128)(2,1)S(1)}, bf16[512,1024]{1,0:T(8,128)(2,1)S(1)}, u32[]{:S(2)}, u32[]{:S(2)}) collective-permute-start(bf16[512,1024]{1,0:T(8,128)(2,1)S(1)} %copy-done.7), channel_id=1, source_target_pairs={{0,1},{1,0},{2,3},{3,2},{4,5},{5,4},{6,7},{7,6},{8,9},{9,8},{10,11... | collective-permute-start | bytes 3145736 | tf_op jit(solution)/shard_map/ppermute | solution.py:652
  26.5 28.9 %collective-permute-start.12 = (bf16[1024,512]{1,0:T(8,128)(2,1)S(1)}, bf16[1024,512]{1,0:T(8,128)(2,1)S(1)}, u32[]{:S(2)}, u32[]{:S(2)}) collective-permute-start(bf16[1024,512]{1,0:T(8,128)(2,1)S(1)} %copy-done.8), channel_id=1, source_target_pairs={{0,1},{1,0},{2,3},{3,2},{4,5},{5,4},{6,7},{7,6},{8,9},{9,8},{10,11... | collective-permute-start | bytes 3145736 | tf_op jit(solution)/shard_map/ppermute | solution.py:652
  88.6 104.2 %collective-permute-start.15 = (bf16[512,512]{1,0:T(8,128)(2,1)S(1)}, bf16[512,512]{1,0:T(8,128)(2,1)S(1)}, u32[]{:S(2)}, u32[]{:S(2)}) collective-permute-start(bf16[512,512]{1,0:T(8,128)(2,1)S(1)} %copy-done.18), channel_id=1, source_target_pairs={{0,1},{1,0},{2,3},{3,2},{4,5},{5,4},{6,7},{7,6},{8,9},{9,8},{10,11... | collective-permute-start | bytes 1572872 | tf_op jit(solution)/shard_map/ppermute | solution.py:652
  94.4 19.2 %collective-permute-start.18 = (bf16[8,160,512]{2,1,0:T(8,128)(2,1)S(1)}, bf16[8,160,512]{2,1,0:T(8,128)(2,1)S(1)}, u32[]{:S(2)}, u32[]{:S(2)}) collective-permute-start(bf16[8,160,512]{2,1,0:T(8,128)(2,1)S(1)} %constant_dynamic-slice_fusion.8.refs_11_), channel_id=1, source_target_pairs={{0,2},{1,5},{2,0},{3,7},{4,6},{5,1},{6,4},{7,3},{8,10},{9,13},{10,... | collective-permute-start | bytes 3932168 | tf_op jit(solution)/shard_map/ppermute | solution.py:684
  113.6 27.3 %collective-permute-start.22 = (bf16[1024,512]{1,0:T(8,128)(2,1)}, bf16[1024,512]{1,0:T(8,128)(2,1)S(1)}, u32[]{:S(2)}, u32[]{:S(2)}) collective-permute-start(bf16[1024,512]{1,0:T(8,128)(2,1)} %get-tuple-element.115), channel_id=1, source_target_pairs={{0,1},{1,0},{2,3},{3,2},{4,5},{5,4},{6,7},{7,6},{8,9},{9,8},{10,11... | collective-permute-start | bytes 3145736 | tf_op jit(solution)/shard_map/ppermute | solution.py:652
  114.1 20.7 %collective-permute-start.19 = (bf16[4,160,512]{2,1,0:T(8,128)(2,1)S(1)}, bf16[4,160,512]{2,1,0:T(8,128)(2,1)S(1)}, u32[]{:S(2)}, u32[]{:S(2)}) collective-permute-start(bf16[4,160,512]{2,1,0:T(8,128)(2,1)S(1)} %constant_dynamic-slice_fusion.7.refs_19_), channel_id=1, source_target_pairs={{0,4},{1,9},{2,6},{3,11},{4,0},{5,13},{6,2},{7,15},{8,12},{9,1},{1... | collective-permute-start | bytes 1966088 | tf_op jit(solution)/shard_map/ppermute | solution.py:684
  140.7 52.2 %collective-permute-start.26 = (bf16[512,512]{1,0:T(8,128)(2,1)}, bf16[512,512]{1,0:T(8,128)(2,1)S(1)}, u32[]{:S(2)}, u32[]{:S(2)}) collective-permute-start(bf16[512,512]{1,0:T(8,128)(2,1)} %get-tuple-element.133), channel_id=1, source_target_pairs={{0,1},{1,0},{2,3},{3,2},{4,5},{5,4},{6,7},{7,6},{8,9},{9,8},{10,11... | collective-permute-start | bytes 1572872 | tf_op jit(solution)/shard_map/ppermute | solution.py:652
  141.3 19.4 %collective-permute-start.24 = (bf16[8,80,512]{2,1,0:T(8,128)(2,1)S(1)}, bf16[8,80,512]{2,1,0:T(8,128)(2,1)S(1)}, u32[]{:S(2)}, u32[]{:S(2)}) collective-permute-start(bf16[8,80,512]{2,1,0:T(8,128)(2,1)S(1)} %constant_dynamic-slice_fusion.5.refs_12_), channel_id=1, source_target_pairs={{0,2},{1,5},{2,0},{3,7},{4,6},{5,1},{6,4},{7,3},{8,10},{9,13},{10,... | collective-permute-start | bytes 1966088 | tf_op jit(solution)/shard_map/ppermute | solution.py:684
  142.6 19.6 %collective-permute-start.21 = (bf16[2,160,512]{2,1,0:T(8,128)(2,1)S(1)}, bf16[2,160,512]{2,1,0:T(8,128)(2,1)S(1)}, u32[]{:S(2)}, u32[]{:S(2)}) collective-permute-start(bf16[2,160,512]{2,1,0:T(8,128)(2,1)S(1)} %add_convert_fusion.9.refs_11_), channel_id=1, source_target_pairs={{0,16},{1,17},{2,18},{3,19},{4,20},{5,21},{6,22},{7,23},{8,24},{9,... | collective-permute-start | bytes 983048 | tf_op jit(solution)/shard_map/ppermute | solution.py:684
  160.6 25.4 %collective-permute-start.27 = (bf16[896,512]{1,0:T(8,128)(2,1)}, bf16[896,512]{1,0:T(8,128)(2,1)S(1)}, u32[]{:S(2)}, u32[]{:S(2)}) collective-permute-start(bf16[896,512]{1,0:T(8,128)(2,1)} %get-tuple-element.135), channel_id=1, source_target_pairs={{0,1},{1,0},{2,3},{3,2},{4,5},{5,4},{6,7},{7,6},{8,9},{9,8},{10,11... | collective-permute-start | bytes 2752520 | tf_op jit(solution)/shard_map/ppermute | solution.py:652
  161.0 23.1 %collective-permute-start.29 = (bf16[4,80,512]{2,1,0:T(8,128)(2,1)S(1)}, bf16[4,80,512]{2,1,0:T(8,128)(2,1)S(1)}, u32[]{:S(2)}, u32[]{:S(2)}) collective-permute-start(bf16[4,80,512]{2,1,0:T(8,128)(2,1)S(1)} %constant_dynamic-slice_fusion.4.refs_11_), channel_id=1, source_target_pairs={{0,4},{1,9},{2,6},{3,11},{4,0},{5,13},{6,2},{7,15},{8,12},{9,1},{1... | collective-permute-start | bytes 983048 | tf_op jit(solution)/shard_map/ppermute | solution.py:684
  162.3 22.4 %collective-permute-start.28 = (bf16[2,160,512]{2,1,0:T(8,128)(2,1)S(1)}, bf16[2,160,512]{2,1,0:T(8,128)(2,1)S(1)}, u32[]{:S(2)}, u32[]{:S(2)}) collective-permute-start(bf16[2,160,512]{2,1,0:T(8,128)(2,1)S(1)} %add_convert_fusion.8.refs_10_), channel_id=1, source_target_pairs={{0,8},{1,3},{2,10},{3,1},{4,12},{5,7},{6,14},{7,5},{8,0},{9,11},{1... | collective-permute-start | bytes 983048 | tf_op jit(solution)/shard_map/ppermute | solution.py:697
  186.1 22.4 %collective-permute-start.42 = (bf16[4,160,512]{2,1,0:T(8,128)(2,1)S(1)}, bf16[4,160,512]{2,1,0:T(8,128)(2,1)S(1)}, u32[]{:S(2)}, u32[]{:S(2)}) collective-permute-start(bf16[4,160,512]{2,1,0:T(8,128)(2,1)S(1)} %bitcast_select_fusion.4), channel_id=1, source_target_pairs={{0,4},{1,9},{2,6},{3,11},{4,0},{5,13},{6,2},{7,15},{8,12},{9,1},{1... | collective-permute-start | bytes 1966088 | tf_op jit(solution)/shard_map/ppermute | solution.py:697
  208.6 34.9 %collective-permute-start.43 = (bf16[8,160,512]{2,1,0:T(8,128)(2,1)S(1)}, bf16[8,160,512]{2,1,0:T(8,128)(2,1)}, u32[]{:S(2)}, u32[]{:S(2)}) collective-permute-start(bf16[8,160,512]{2,1,0:T(8,128)(2,1)S(1)} %bitcast_select_fusion), channel_id=1, source_target_pairs={{0,2},{1,5},{2,0},{3,7},{4,6},{5,1},{6,4},{7,3},{8,10},{9,13},{10,... | collective-permute-start | bytes 3932168 | tf_op jit(solution)/shard_map/ppermute | solution.py:697
  220.6 17.6 %collective-permute-start.41 = (bf16[8,80,512]{2,1,0:T(8,128)(2,1)}, bf16[8,80,512]{2,1,0:T(8,128)(2,1)}, u32[]{:S(2)}, u32[]{:S(2)}) collective-permute-start(bf16[8,80,512]{2,1,0:T(8,128)(2,1)} %bitcast_select_fusion.2), channel_id=1, source_target_pairs={{0,2},{1,5},{2,0},{3,7},{4,6},{5,1},{6,4},{7,3},{8,10},{9,13},{10,... | collective-permute-start | bytes 1966088 | tf_op jit(solution)/shard_map/ppermute | solution.py:697
  237.2 11.1 %collective-permute-start.36 = (bf16[8,56,512]{2,1,0:T(8,128)(2,1)S(1)}, bf16[8,56,512]{2,1,0:T(8,128)(2,1)S(1)}, u32[]{:S(2)}, u32[]{:S(2)}) collective-permute-start(bf16[8,56,512]{2,1,0:T(8,128)(2,1)S(1)} %bitcast_select_fusion.5), channel_id=1, source_target_pairs={{0,2},{1,5},{2,0},{3,7},{4,6},{5,1},{6,4},{7,3},{8,10},{9,13},{10,... | collective-permute-start | bytes 1376264 | tf_op jit(solution)/shard_map/ppermute | solution.py:697
  (48 other events, 328.7 us)
where the time goes:
time: 257 us; the launch traced here: 253 us
  Pallas kernels  164 us (64%)
  waiting for transfers between devices  34.7 us (14%)
  starting transfers between devices  31 us (12%)
  other arithmetic  16 us (6%)
  local copies, waits for them, and re-layouts  5.98 us (2%)
    pallas_call x13, Pallas kernels, staged_call(): pl.pallas_call(kernel, out_shape=[pltpu.HBM(s, d) for s, d, _ in outs] +...  164 us
    ppermute x12, starting transfers between devices, scatter(): got = lax.ppermute(self.away, ('dp', 'tensor'), self.plan[self.step][0])  16.6 us
    ppermute x12, waiting for transfers between devices, scatter(): got = lax.ppermute(self.away, ('dp', 'tensor'), self.plan[self.step][0])  16 us
    ppermute x9, waiting for transfers between devices, gather(): got = lax.ppermute(self.x, ('dp', 'tensor'), pairs)  14.6 us
    ppermute x9, starting transfers between devices, gather(): got = lax.ppermute(self.x, ('dp', 'tensor'), pairs)  7.82 us
    select_n x9, other arithmetic, gather(): jnp.where(first, self.x[None], got[None])  6.7 us
    ppermute x23, starting transfers between devices, swap(): return lax.ppermute(x, 'tensor', [(0, 1), (1, 0)])  6.57 us
  transfers between devices with their start and end apart: 44, of which 10 were waited for; matrix products, arithmetic and copies ran while one was open for 7% of the time, Pallas kernels for 54%

commit v1 on v0

--- a/solution.py
+++ b/solution.py
@@ -94,7 +94,7 @@
         return self.near
 
 
-def staged_call(body, scalars, big_ins, small_ins, outs, small_outs=(), scratch=(), after=(), micros=10.0):
+def staged_call(body, scalars, big_ins, small_ins, outs, small_outs=(), scratch=(), after=(), micros=10.0, pinned=False):
     def shape_of(a, part):
         if part is None:
             return a.shape
@@ -127,7 +127,8 @@
     held += [(one.shape, one.dtype) for one in scratch]
     size = sum(math.prod(s) * jnp.dtype(d).itemsize for s, d in held)
     far = [pltpu.with_memory_space_constraint(a, pltpu.HBM) for a, _ in big_ins]
-    small_ins = [pltpu.with_memory_space_constraint(a, pltpu.HBM) for a in small_ins]
+    if pinned:
+        small_ins = [pltpu.with_memory_space_constraint(a, pltpu.HBM) for a in small_ins]
     return pl.pallas_call(
         kernel,
         out_shape=[pltpu.HBM(s, d) for s, d, _ in outs] + [jax.ShapeDtypeStruct(s, d) for s, d in small_outs],
@@ -691,13 +692,15 @@
         if self.done:
             self.step -= 1
 
-    def gather(self, last):
+    def gather(self, last, *beside):
         while self.step > last:
             pairs, bit = self.plan[self.step - 1]
             got = lax.ppermute(self.x, ("dp", "tensor"), pairs)
             self.step -= 1
             if self.step == 0:
                 return self.x, got
+            if beside and self.step == last:
+                got = lax.optimization_barrier((got, *beside))[0]
             first = lax.broadcasted_iota(jnp.int32, (2,) + self.x.shape, 0) == bit
             self.x = jnp.where(first, self.x[None], got[None]).reshape((2 * self.x.shape[0],) + self.x.shape[1:])
 
@@ -741,7 +744,7 @@
     qa, ka, va, ctx, y1, h1 = staged_call(
         functools.partial(attend_forward, False), core,
         [(tokens, "core"), (tokens_t, "core"), (self_qkv, None), (self_qkv_t, None), (self_out, None), (self_out_t, None)],
-        [self_bias, self_bias_t, self_out_bias, norm_gain, norm_bias, dec_segment], forward_outs, micros=18)
+        [self_bias, self_bias_t, self_out_bias, norm_gain, norm_bias, dec_segment], forward_outs, micros=18, pinned=True)
     qa2, ka2, va2, ctx2, y2, h2 = staged_call(
         functools.partial(attend_forward, True), core,
         [(h1, None), (memory, "core"), (memory_t, "core"), (cross_qkv, None), (cross_qkv_t, None), (cross_out, None),
@@ -835,7 +838,10 @@
     grad_memory = together(dmem_m, dmem_t)
     g3_got = lax.optimization_barrier((swap(sides[1][0]), sum1.x, sum2.away))[0]
     sum3 = RowSum(packed(added(sides[0][0], g3_got)), dp_size, dp_index, core_index)
-    dx_m, dx_t = staged_call(input_gradient, core, sides[0][1] + sides[1][1] + [(dy1, None)], [], [half_out, half_out], micros=5)
+    dx_m, dx_t = staged_call(input_gradient, core, sides[0][1] + sides[1][1] + [(dy1, None)], [], [half_out, half_out],
+                             after=[sum3.away], micros=5)
+    sum2.scatter(sum3.away)
+    sum3.scatter(dx_m)
     sum3.scatter(output, slot_states, grad_memory)
     while not sum2.done:
         sum2.scatter()
@@ -857,6 +863,7 @@
     grad_cross_qkv, grad_cross_out, grad_self_out = staged_call(
         unpack_cross, scalars, halves, [], [qkv_out, ((hw, width), f32, 1), ((hw, width), f32, 1)],
         scratch=[pltpu.VMEM((5 * hw, width), bf16)], micros=3)
+    sum3.gather(1, grad_ffn_out)
     scalars, halves = ends(sum3)
     (grad_self_qkv, grad_self_bias, grad_self_out_bias, grad_cross_bias, grad_cross_out_bias, grad_ffn_in_bias,
      grad_ffn_out_bias, grad_norm_gain, grad_norm_bias, grad_slot_bias) = staged_call(

time: 257 us -> 247 us (0.961)
  waiting for transfers between devices: 34.7 us -> 29.1 us
  Pallas kernels: 164 us -> 159 us
  starting transfers between devices: 31 us -> 35.5 us
  other arithmetic: 16 us -> 13.3 us
    ppermute x12, waiting for transfers between devices: 16 us -> 9.31 us  [scatter(): got = lax.ppermute(self.away, ('dp', 'tensor'), self.plan[self.step][0])]
    pallas_call x13, Pallas kernels: 164 us -> 159 us  [staged_call(): pl.pallas_call(kernel, out_shape=[pltpu.HBM(s, d) for s, d, _ in outs] +...]
  transfers between devices with their start and end apart: 44 -> 44, of which waited for: 10 -> 10; matrix products, arithmetic and copies ran while one was open for 7% -> 6% of each run, Pallas kernels for 54% -> 54%
where the time goes in v1:
time: 247 us; the launch traced here: 244 us
  Pallas kernels  159 us (64%)
  starting transfers between devices  35.5 us (14%)
  waiting for transfers between devices  29.1 us (12%)
  other arithmetic  13.3 us (5%)
  local copies, waits for them, and re-layouts  5.38 us (2%)
    pallas_call x13, Pallas kernels, staged_call(): pl.pallas_call(kernel, out_shape=[pltpu.HBM(s, d) for s, d, _ in outs] +...  159 us
    ppermute x12, starting transfers between devices, scatter(): got = lax.ppermute(self.away, ('dp', 'tensor'), self.plan[self.step][0])  19.1 us
    ppermute x9, waiting for transfers between devices, gather(): got = lax.ppermute(self.x, ('dp', 'tensor'), pairs)  16 us
    ppermute x9, starting transfers between devices, gather(): got = lax.ppermute(self.x, ('dp', 'tensor'), pairs)  10.4 us
    ppermute x12, waiting for transfers between devices, scatter(): got = lax.ppermute(self.away, ('dp', 'tensor'), self.plan[self.step][0])  9.31 us
    ppermute x23, starting transfers between devices, swap(): return lax.ppermute(x, 'tensor', [(0, 1), (1, 0)])  5.98 us
  transfers between devices with their start and end apart: 44, of which 10 were waited for; matrix products, arithmetic and copies ran while one was open for 6% of the time, Pallas kernels for 54%

profile of v1, /device:TPU:0, one launch (start us, length us, event | category | flops | bytes accessed | tf_op | source)
XLA Modules:
  0.0 243.9 jit_solution(2134517369693079041)
XLA Ops:
  2.2 3.0 %collective-permute-done.14.refs_19_.refs_6_ = bf16[256]{0:T(256)(128)(2,1)S(1)} collective-permute-done((bf16[256]{0:T(256)(128)(2,1)}, bf16[256]{0:T(256)(128)(2,1)S(1)}, u32[]{:S(2)}, u32[]{:S(2)}) %collective-permute-start.14) | collective-permute-done | bytes 544 | tf_op jit(solution)/shard_map/ppermute | solution.py:653
  7.4 17.8 %shard_map.374 = (bf16[8,80,1024]{2,1,0:T(8,128)(2,1)}, bf16[8,80,1024]{2,1,0:T(8,128)(2,1)}, bf16[8,80,1024]{2,1,0:T(8,128)(2,1)}, bf16[512,1024]{1,0:T(8,128)(...) custom-call(s32[1]{0:T(128)} %bitcast.refs_0_, bf16[2,512,512]{2,1,0:T(8,128)(2,1)} %refs_2_.5, ...), custom_call_target="tpu_custom_call" | custom-call | flops 19800000512 | bytes 1024 | tf_op jit(solution)/shard_map/pallas_call | solution.py:132
  27.5 27.0 %shard_map.375 = (bf16[8,80,1024]{2,1,0:T(8,128)(2,1)}, bf16[8,80,1024]{2,1,0:T(8,128)(2,1)}, bf16[8,80,1024]{2,1,0:T(8,128)(2,1)}, bf16[512,1024]{1,0:T(8,128)(...) custom-call(s32[1]{0:T(128)} %bitcast.refs_0_, bf16[1024,512]{1,0:T(8,128)(2,1)} %get-tuple-element.90.refs_1_.refs_2_, ...), custom_call_target="tpu_custom_call" | custom-call | flops 19800000512 | bytes 1024 | tf_op jit(solution)/shard_map/pallas_call | solution.py:132
  56.5 24.7 %shard_map.376 = (bf16[512,512]{1,0:T(8,128)(2,1)}, bf16[512,512]{1,0:T(8,128)(2,1)}, f32[1024,512]{1,0:T(8,128)}, bf16[1024,512]{1,0:T(8,128)(2,1)}, bf16[2560,...) custom-call(s32[1]{0:T(128)} %bitcast.refs_0_, ...), custom_call_target="tpu_custom_call" | custom-call | flops 27499999232 | bytes 1024 | tf_op jit(solution)/shard_map/pallas_call | solution.py:132
  81.6 4.9 %shard_map.377 = (bf16[512,256]{1,0:T(8,128)(2,1)}, bf16[512,256]{1,0:T(8,128)(2,1)}) custom-call(s32[1]{0:T(128)} %bitcast.refs_0_, bf16[512,512]{1,0:T(8,128)(2,1)} %get-tuple-element.93.refs_1_, bf16[512,512]{1,0:T(8,128)(2,1)} %get-tuple-element.94.refs_2_, bf16[1024,256]{1,0:T(8,128)(2,1)} %refs_3_.8, bf16[1024,256]{1,0:T(8,128)(2,1)} %copy-done.36, ...), custom_call_target="tpu_custom_call" | custom-call | flops 4400000000 | bytes 1024 | tf_op jit(solution)/shard_map/pallas_call | solution.py:132
  90.2 2.5 %add_convert_fusion = bf16[2560,512]{1,0:T(8,128)(2,1)S(1)} fusion(bf16[2560,512]{1,0:T(8,128)(2,1)} %collective-permute-done.17, bf16[2560,512]{1,0:T(8,128)(2,1)S(1)} %copy-done.17), kind=kLoop, calls=%fused_computation | loop fusion | flops 5242880 | bytes 7864320 | tf_op jit(solution)/shard_map/convert_element_type | solution.py:772
  92.9 2.8 %collective-permute-start.18 = (bf16[8,160,512]{2,1,0:T(8,128)(2,1)S(1)}, bf16[8,160,512]{2,1,0:T(8,128)(2,1)S(1)}, u32[]{:S(2)}, u32[]{:S(2)}) collective-permute-start(bf16[8,160,512]{2,1,0:T(8,128)(2,1)S(1)} %constant_dynamic-slice_fusion.8.refs_11_), channel_id=1, source_target_pairs={{0,2},{1,5},{2,0},{3,7},{4,6},{5,1},{6,4},{7,3},{8,10},{9,13},{10,... | collective-permute-start | bytes 3932168 | tf_op jit(solution)/shard_map/ppermute | solution.py:685
  95.7 15.6 %shard_map.378 = (bf16[1024,512]{1,0:T(8,128)(2,1)}, f32[16,512]{1,0:T(8,128)}, bf16[256,1024]{1,0:T(8,128)(2,1)}, bf16[256,1024]{1,0:T(8,128)(2,1)}, bf16[256,1024]{1,0:T(8,128)(2,1)}) custom-call(s32[1]{0:T(128)} %bitcast.refs_0_, bf16[1024,512]{1,0:T(8,128)(2,1)} %get-tuple-element.97.refs_1_, bf16[1024,512]{1,0:T(8,128)(2,1)} %get-tuple-element.90.refs_1_.refs_2_, ...), custom_call_target="tpu_custom_call" | custom-call | flops 16499999744 | bytes 1024 | tf_op jit(solution)/shard_map/pallas_call | solution.py:132
  113.9 18.0 %shard_map.379 = (bf16[1280,512]{1,0:T(8,128)(2,1)}, f32[16,512]{1,0:T(8,128)}, f32[16,512]{1,0:T(8,128)}, bf16[256,1024]{1,0:T(8,128)(2,1)}, bf16[256,1024]{1,0...) custom-call(s32[1]{0:T(128)} %bitcast.refs_0_, ...), custom_call_target="tpu_custom_call" | custom-call | flops 18699999232 | bytes 1024 | tf_op jit(solution)/shard_map/pallas_call | solution.py:132
  133.9 4.3 %shard_map.380 = (bf16[512,512]{1,0:T(8,128)(2,1)}, bf16[512,512]{1,0:T(8,128)(2,1)}) custom-call(s32[1]{0:T(128)} %bitcast.refs_0_, bf16[256,1024]{1,0:T(8,128)(2,1)} %get-tuple-element.120.refs_1_, bf16[256,1024]{1,0:T(8,128)(2,1)} %get-tuple-element.121.refs_2_, bf16[3,512,256]{2,1,0:T(8,128)(2,1)} %refs_3_.11, ...), custom_call_target="tpu_custom_call" | custom-call | flops 4400000000 | bytes 1024 | tf_op jit(solution)/shard_map/pallas_call | solution.py:132
  140.3 2.6 %collective-permute-start.21 = (bf16[2,160,512]{2,1,0:T(8,128)(2,1)S(1)}, bf16[2,160,512]{2,1,0:T(8,128)(2,1)S(1)}, u32[]{:S(2)}, u32[]{:S(2)}) collective-permute-start(bf16[2,160,512]{2,1,0:T(8,128)(2,1)S(1)} %add_convert_fusion.9.refs_11_), channel_id=1, source_target_pairs={{0,16},{1,17},{2,18},{3,19},{4,20},{5,21},{6,22},{7,23},{8,24},{9,... | collective-permute-start | bytes 983048 | tf_op jit(solution)/shard_map/ppermute | solution.py:685
  143.0 14.6 %shard_map.382 = (bf16[896,512]{1,0:T(8,128)(2,1)}, bf16[256,1024]{1,0:T(8,128)(2,1)}, bf16[256,1024]{1,0:T(8,128)(2,1)}, bf16[256,1024]{1,0:T(8,128)(2,1)}) custom-call(s32[1]{0:T(128)} %bitcast.refs_0_, bf16[1024,512]{1,0:T(8,128)(2,1)} %get-tuple-element.112.refs_1_, bf16[2,512,512]{2,1,0:T(8,128)(2,1)} %refs_2_.5, bf16[2,512,512]{2,1,0:T(8,128)(2,1)} %copy-done.25, ...), custom_call_target="tpu_custom_call" | custom-call | flops 16499999744 | bytes 1024 | tf_op jit(solution)/shard_map/pallas_call | solution.py:132
  160.1 14.6 %shard_map.381 = (bf16[896,512]{1,0:T(8,128)(2,1)}, bf16[256,1024]{1,0:T(8,128)(2,1)}, bf16[256,1024]{1,0:T(8,128)(2,1)}, bf16[256,1024]{1,0:T(8,128)(2,1)}) custom-call(s32[1]{0:T(128)} %bitcast.refs_0_, bf16[1024,512]{1,0:T(8,128)(2,1)} %get-tuple-element.112.refs_1_, bf16[2,512,512]{2,1,0:T(8,128)(2,1)} %refs_2_.5, bf16[2,512,512]{2,1,0:T(8,128)(2,1)} %copy-done.25, ...), custom_call_target="tpu_custom_call" | custom-call | flops 16499999744 | bytes 1024 | tf_op jit(solution)/shard_map/pallas_call | solution.py:132
  178.8 5.7 %shard_map.383 = (bf16[512,512]{1,0:T(8,128)(2,1)}, bf16[512,512]{1,0:T(8,128)(2,1)}) custom-call(s32[1]{0:T(128)} %bitcast.refs_0_, bf16[256,1024]{1,0:T(8,128)(2,1)} %get-tuple-element.126.refs_1_, bf16[256,1024]{1,0:T(8,128)(2,1)} %get-tuple-element.127.refs_2_, bf16[256,1024]{1,0:T(8,128)(2,1)} %get-tuple-element.128.refs_3_, ...), custom_call_target="tpu_custom_call" | custom-call | flops 5500000256 | bytes 1024 | tf_op jit(solution)/shard_map/pallas_call | solution.py:132
  184.7 6.9 %collective-permute-done.36 = bf16[4,160,512]{2,1,0:T(8,128)(2,1)S(1)} collective-permute-done((bf16[4,160,512]{2,1,0:T(8,128)(2,1)S(1)}, bf16[4,160,512]{2,1,0:T(8,128)(2,1)S(1)}, u32[]{:S(2)}, u32[]{:S(2)}) %collective-permute-start.36) | collective-permute-done | bytes 655392 | tf_op jit(solution)/shard_map/ppermute | solution.py:698
  196.5 5.4 %collective-permute-done.31 = bf16[4,56,512]{2,1,0:T(8,128)(2,1)S(1)} collective-permute-done((bf16[4,56,512]{2,1,0:T(8,128)(2,1)S(1)}, bf16[4,56,512]{2,1,0:T(8,128)(2,1)S(1)}, u32[]{:S(2)}, u32[]{:S(2)}) %collective-permute-start.31) | collective-permute-done | bytes 229408 | tf_op jit(solution)/shard_map/ppermute | solution.py:685
  204.2 2.7 %collective-permute-done.32 = bf16[2,56,512]{2,1,0:T(8,128)(2,1)S(1)} collective-permute-done((bf16[2,56,512]{2,1,0:T(8,128)(2,1)S(1)}, bf16[2,56,512]{2,1,0:T(8,128)(2,1)S(1)}, u32[]{:S(2)}, u32[]{:S(2)}) %collective-permute-start.32) | collective-permute-done | bytes 114720 | tf_op jit(solution)/shard_map/ppermute | solution.py:685
  206.9 2.6 %collective-permute-start.33 = (bf16[2,56,512]{2,1,0:T(8,128)(2,1)S(1)}, bf16[2,56,512]{2,1,0:T(8,128)(2,1)S(1)}, u32[]{:S(2)}, u32[]{:S(2)}) collective-permute-start(bf16[2,56,512]{2,1,0:T(8,128)(2,1)S(1)} %add_convert_fusion.14), channel_id=1, source_target_pairs={{0,16},{1,17},{2,18},{3,19},{4,20},{5,21},{6,22},{7,23},{8,24},{9,... | collective-permute-start | bytes 344072 | tf_op jit(solution)/shard_map/ppermute | solution.py:685
  212.9 2.9 %collective-permute-start.34 = (bf16[2,56,512]{2,1,0:T(8,128)(2,1)S(1)}, bf16[2,56,512]{2,1,0:T(8,128)(2,1)S(1)}, u32[]{:S(2)}, u32[]{:S(2)}) collective-permute-start(bf16[2,56,512]{2,1,0:T(8,128)(2,1)S(1)} %add_convert_fusion.13), channel_id=1, source_target_pairs={{0,8},{1,3},{2,10},{3,1},{4,12},{5,7},{6,14},{7,5},{8,0},{9,11},{1... | collective-permute-start | bytes 344072 | tf_op jit(solution)/shard_map/ppermute | solution.py:698
  215.9 2.2 collective-permute-done.42
  222.5 4.7 %shard_map.384 = (f32[1024,256]{1,0:T(8,128)}, f32[512,1024]{1,0:T(8,128)}, f32[1024,512]{1,0:T(8,128)}) custom-call(s32[2]{0:T(128)S(1)} %pad_add_fusion.refs_0_, bf16[1280,512]{1,0:T(8,128)(2,1)} %bitcast_select_fusion.1.refs_1_, bf16[1280,512]{1,0:T(8,128)(2,1)} %bitcast.14.refs_2_), custom_call_target="tpu_custom_call" | custom-call | flops 4400000000 | bytes 1024 | tf_op jit(solution)/shard_map/pallas_call | solution.py:132
  227.3 3.4 %collective-permute-done.35 = bf16[4,56,512]{2,1,0:T(8,128)(2,1)S(1)} collective-permute-done((bf16[4,56,512]{2,1,0:T(8,128)(2,1)S(1)}, bf16[4,56,512]{2,1,0:T(8,128)(2,1)S(1)}, u32[]{:S(2)}, u32[]{:S(2)}) %collective-permute-start.35) | collective-permute-done | bytes 229408 | tf_op jit(solution)/shard_map/ppermute | solution.py:698
  232.7 3.5 %shard_map.386 = (f32[3,512,256]{2,1,0:T(8,128)}, f32[256,512]{1,0:T(8,128)}, f32[256,512]{1,0:T(8,128)}) custom-call(s32[2]{0:T(128)S(1)} %pad_add_fusion.refs_0_, bf16[640,512]{1,0:T(8,128)(2,1)} %bitcast_select_fusion.3.refs_1_, bf16[640,512]{1,0:T(8,128)(2,1)} %bitcast.25.refs_2_), custom_call_target="tpu_custom_call" | custom-call | flops 3300000000 | bytes 1024 | tf_op jit(solution)/shard_map/pallas_call | solution.py:132
  240.0 3.6 %shard_map.385 = (f32[3,512,256]{2,1,0:T(8,128)}, f32[2,256]{1,0:T(2,128)}, f32[512]{0:T(512)}, f32[2,256]{1,0:T(2,128)}, f32[512]{0:T(512)}, /*index=5*/f32[102...) custom-call(s32[2]{0:T(128)S(1)} %pad_add_fusion.refs_0_, ...), custom_call_target="tpu_custom_call" | custom-call | flops 3300000000 | bytes 1024 | tf_op jit(solution)/shard_map/pallas_call | solution.py:132
  (212 shorter events, 46.2 us)
Async XLA Ops:
  5.2 21.3 %collective-permute-start.7 = (bf16[2,512,512]{2,1,0:T(8,128)(2,1)}, bf16[2,512,512]{2,1,0:T(8,128)(2,1)S(1)}, u32[]{:S(2)}, u32[]{:S(2)}) collective-permute-start(bf16[2,512,512]{2,1,0:T(8,128)(2,1)} %refs_3_.10), channel_id=1, source_target_pairs={{0,1},{1,0},{2,3},{3,2},{4,5},{5,4},{6,7},{7,6},{8,9},{9,8},{10,11... | collective-permute-start | bytes 3145736 | tf_op jit(solution)/shard_map/ppermute | solution.py:653
  5.6 20.6 %collective-permute-start.8 = (bf16[3,512,256]{2,1,0:T(8,128)(2,1)}, bf16[3,512,256]{2,1,0:T(8,128)(2,1)S(1)}, u32[]{:S(2)}, u32[]{:S(2)}) collective-permute-start(bf16[3,512,256]{2,1,0:T(8,128)(2,1)} %refs_3_.11), channel_id=1, source_target_pairs={{0,1},{1,0},{2,3},{3,2},{4,5},{5,4},{6,7},{7,6},{8,9},{9,8},{10,11... | collective-permute-start | bytes 2359304 | tf_op jit(solution)/shard_map/ppermute | solution.py:653
  5.7 20.2 %collective-permute-start.9 = (bf16[256,512]{1,0:T(8,128)(2,1)}, bf16[256,512]{1,0:T(8,128)(2,1)S(1)}, u32[]{:S(2)}, u32[]{:S(2)}) collective-permute-start(bf16[256,512]{1,0:T(8,128)(2,1)} %refs_5_.7), channel_id=1, source_target_pairs={{0,1},{1,0},{2,3},{3,2},{4,5},{5,4},{6,7},{7,6},{8,9},{9,8},{10,11... | collective-permute-start | bytes 786440 | tf_op jit(solution)/shard_map/ppermute | solution.py:653
  6.1 19.1 %collective-permute-start.10 = (bf16[2,256]{1,0:T(2,128)(2,1)}, bf16[2,256]{1,0:T(2,128)(2,1)S(1)}, u32[]{:S(2)}, u32[]{:S(2)}) collective-permute-start(bf16[2,256]{1,0:T(2,128)(2,1)} %refs_8_.2), channel_id=1, source_target_pairs={{0,1},{1,0},{2,3},{3,2},{4,5},{5,4},{6,7},{7,6},{8,9},{9,8},{10,11... | collective-permute-start | bytes 3080 | tf_op jit(solution)/shard_map/ppermute | solution.py:653
  6.2 19.3 %collective-permute-start.13 = (bf16[1024]{0:T(1024)(128)(2,1)}, bf16[1024]{0:T(1024)(128)(2,1)S(1)}, u32[]{:S(2)}, u32[]{:S(2)}) collective-permute-start(bf16[1024]{0:T(1024)(128)(2,1)} %refs_13_.4), channel_id=1, source_target_pairs={{0,1},{1,0},{2,3},{3,2},{4,5},{5,4},{6,7},{7,6},{8,9},{9,8},{10,11... | collective-permute-start | bytes 6152 | tf_op jit(solution)/shard_map/ppermute | solution.py:653
  25.2 29.3 %collective-permute-start.1 = (bf16[1024,256]{1,0:T(8,128)(2,1)S(1)}, bf16[1024,256]{1,0:T(8,128)(2,1)S(1)}, u32[]{:S(2)}, u32[]{:S(2)}) collective-permute-start(bf16[1024,256]{1,0:T(8,128)(2,1)S(1)} %copy-done.33), channel_id=1, source_target_pairs={{0,1},{1,0},{2,3},{3,2},{4,5},{5,4},{6,7},{7,6},{8,9},{9,8},{10,11... | collective-permute-start | bytes 1572872 | tf_op jit(solution)/shard_map/ppermute | solution.py:653
  25.5 29.0 %collective-permute-start.11 = (bf16[512,1024]{1,0:T(8,128)(2,1)S(1)}, bf16[512,1024]{1,0:T(8,128)(2,1)S(1)}, u32[]{:S(2)}, u32[]{:S(2)}) collective-permute-start(bf16[512,1024]{1,0:T(8,128)(2,1)S(1)} %copy-done.23), channel_id=1, source_target_pairs={{0,1},{1,0},{2,3},{3,2},{4,5},{5,4},{6,7},{7,6},{8,9},{9,8},{10,11... | collective-permute-start | bytes 3145736 | tf_op jit(solution)/shard_map/ppermute | solution.py:653
  25.9 28.7 %collective-permute-start.12 = (bf16[1024,512]{1,0:T(8,128)(2,1)S(1)}, bf16[1024,512]{1,0:T(8,128)(2,1)S(1)}, u32[]{:S(2)}, u32[]{:S(2)}) collective-permute-start(bf16[1024,512]{1,0:T(8,128)(2,1)S(1)} %copy-done.24), channel_id=1, source_target_pairs={{0,1},{1,0},{2,3},{3,2},{4,5},{5,4},{6,7},{7,6},{8,9},{9,8},{10,11... | collective-permute-start | bytes 3145736 | tf_op jit(solution)/shard_map/ppermute | solution.py:653
  26.2 28.4 %collective-permute-start.2 = (bf16[2,512,512]{2,1,0:T(8,128)(2,1)S(1)}, bf16[2,512,512]{2,1,0:T(8,128)(2,1)S(1)}, u32[]{:S(2)}, u32[]{:S(2)}) collective-permute-start(bf16[2,512,512]{2,1,0:T(8,128)(2,1)S(1)} %copy-done.22), channel_id=1, source_target_pairs={{0,1},{1,0},{2,3},{3,2},{4,5},{5,4},{6,7},{7,6},{8,9},{9,8},{10,11... | collective-permute-start | bytes 3145736 | tf_op jit(solution)/shard_map/ppermute | solution.py:653
  26.5 28.0 %collective-permute-start = (bf16[2,512,256]{2,1,0:T(8,128)(2,1)S(1)}, bf16[2,512,256]{2,1,0:T(8,128)(2,1)S(1)}, u32[]{:S(2)}, u32[]{:S(2)}) collective-permute-start(bf16[2,512,256]{2,1,0:T(8,128)(2,1)S(1)} %copy-done.32), channel_id=1, source_target_pairs={{0,1},{1,0},{2,3},{3,2},{4,5},{5,4},{6,7},{7,6},{8,9},{9,8},{10,11... | collective-permute-start | bytes 1572872 | tf_op jit(solution)/shard_map/ppermute | solution.py:653
  87.2 106.1 %collective-permute-start.15 = (bf16[512,512]{1,0:T(8,128)(2,1)S(1)}, bf16[512,512]{1,0:T(8,128)(2,1)S(1)}, u32[]{:S(2)}, u32[]{:S(2)}) collective-permute-start(bf16[512,512]{1,0:T(8,128)(2,1)S(1)} %copy-done.34), channel_id=1, source_target_pairs={{0,1},{1,0},{2,3},{3,2},{4,5},{5,4},{6,7},{7,6},{8,9},{9,8},{10,11... | collective-permute-start | bytes 1572872 | tf_op jit(solution)/shard_map/ppermute | solution.py:653
  92.9 18.5 %collective-permute-start.18 = (bf16[8,160,512]{2,1,0:T(8,128)(2,1)S(1)}, bf16[8,160,512]{2,1,0:T(8,128)(2,1)S(1)}, u32[]{:S(2)}, u32[]{:S(2)}) collective-permute-start(bf16[8,160,512]{2,1,0:T(8,128)(2,1)S(1)} %constant_dynamic-slice_fusion.8.refs_11_), channel_id=1, source_target_pairs={{0,2},{1,5},{2,0},{3,7},{4,6},{5,1},{6,4},{7,3},{8,10},{9,13},{10,... | collective-permute-start | bytes 3932168 | tf_op jit(solution)/shard_map/ppermute | solution.py:685
  111.3 26.9 %collective-permute-start.22 = (bf16[1024,512]{1,0:T(8,128)(2,1)}, bf16[1024,512]{1,0:T(8,128)(2,1)S(1)}, u32[]{:S(2)}, u32[]{:S(2)}) collective-permute-start(bf16[1024,512]{1,0:T(8,128)(2,1)} %get-tuple-element.118), channel_id=1, source_target_pairs={{0,1},{1,0},{2,3},{3,2},{4,5},{5,4},{6,7},{7,6},{8,9},{9,8},{10,11... | collective-permute-start | bytes 3145736 | tf_op jit(solution)/shard_map/ppermute | solution.py:653
  111.9 20.1 %collective-permute-start.19 = (bf16[4,160,512]{2,1,0:T(8,128)(2,1)S(1)}, bf16[4,160,512]{2,1,0:T(8,128)(2,1)S(1)}, u32[]{:S(2)}, u32[]{:S(2)}) collective-permute-start(bf16[4,160,512]{2,1,0:T(8,128)(2,1)S(1)} %constant_dynamic-slice_fusion.7.refs_19_), channel_id=1, source_target_pairs={{0,4},{1,9},{2,6},{3,11},{4,0},{5,13},{6,2},{7,15},{8,12},{9,1},{1... | collective-permute-start | bytes 1966088 | tf_op jit(solution)/shard_map/ppermute | solution.py:685
  138.6 19.2 %collective-permute-start.24 = (bf16[8,80,512]{2,1,0:T(8,128)(2,1)S(1)}, bf16[8,80,512]{2,1,0:T(8,128)(2,1)S(1)}, u32[]{:S(2)}, u32[]{:S(2)}) collective-permute-start(bf16[8,80,512]{2,1,0:T(8,128)(2,1)S(1)} %constant_dynamic-slice_fusion.5.refs_12_), channel_id=1, source_target_pairs={{0,2},{1,5},{2,0},{3,7},{4,6},{5,1},{6,4},{7,3},{8,10},{9,13},{10,... | collective-permute-start | bytes 1966088 | tf_op jit(solution)/shard_map/ppermute | solution.py:685
  140.2 54.4 %collective-permute-start.29 = (bf16[512,512]{1,0:T(8,128)(2,1)S(1)}, bf16[512,512]{1,0:T(8,128)(2,1)S(1)}, u32[]{:S(2)}, u32[]{:S(2)}) collective-permute-start(bf16[512,512]{1,0:T(8,128)(2,1)S(1)} %copy-done.35), channel_id=1, source_target_pairs={{0,1},{1,0},{2,3},{3,2},{4,5},{5,4},{6,7},{7,6},{8,9},{9,8},{10,11... | collective-permute-start | bytes 1572872 | tf_op jit(solution)/shard_map/ppermute | solution.py:653
  140.3 18.5 %collective-permute-start.21 = (bf16[2,160,512]{2,1,0:T(8,128)(2,1)S(1)}, bf16[2,160,512]{2,1,0:T(8,128)(2,1)S(1)}, u32[]{:S(2)}, u32[]{:S(2)}) collective-permute-start(bf16[2,160,512]{2,1,0:T(8,128)(2,1)S(1)} %add_convert_fusion.9.refs_11_), channel_id=1, source_target_pairs={{0,16},{1,17},{2,18},{3,19},{4,20},{5,21},{6,22},{7,23},{8,24},{9,... | collective-permute-start | bytes 983048 | tf_op jit(solution)/shard_map/ppermute | solution.py:685
  157.6 19.9 %collective-permute-start.25 = (bf16[896,512]{1,0:T(8,128)(2,1)}, bf16[896,512]{1,0:T(8,128)(2,1)S(1)}, u32[]{:S(2)}, u32[]{:S(2)}) collective-permute-start(bf16[896,512]{1,0:T(8,128)(2,1)} %get-tuple-element.135), channel_id=1, source_target_pairs={{0,1},{1,0},{2,3},{3,2},{4,5},{5,4},{6,7},{7,6},{8,9},{9,8},{10,11... | collective-permute-start | bytes 2752520 | tf_op jit(solution)/shard_map/ppermute | solution.py:653
  158.1 16.6 %collective-permute-start.27 = (bf16[4,80,512]{2,1,0:T(8,128)(2,1)S(1)}, bf16[4,80,512]{2,1,0:T(8,128)(2,1)S(1)}, u32[]{:S(2)}, u32[]{:S(2)}) collective-permute-start(bf16[4,80,512]{2,1,0:T(8,128)(2,1)S(1)} %constant_dynamic-slice_fusion.4.refs_11_), channel_id=1, source_target_pairs={{0,4},{1,9},{2,6},{3,11},{4,0},{5,13},{6,2},{7,15},{8,12},{9,1},{1... | collective-permute-start | bytes 983048 | tf_op jit(solution)/shard_map/ppermute | solution.py:685
  158.9 17.0 %collective-permute-start.26 = (bf16[2,160,512]{2,1,0:T(8,128)(2,1)S(1)}, bf16[2,160,512]{2,1,0:T(8,128)(2,1)S(1)}, u32[]{:S(2)}, u32[]{:S(2)}) collective-permute-start(bf16[2,160,512]{2,1,0:T(8,128)(2,1)S(1)} %add_convert_fusion.8.refs_10_), channel_id=1, source_target_pairs={{0,8},{1,3},{2,10},{3,1},{4,12},{5,7},{6,14},{7,5},{8,0},{9,11},{1... | collective-permute-start | bytes 983048 | tf_op jit(solution)/shard_map/ppermute | solution.py:698
  176.0 15.6 %collective-permute-start.36 = (bf16[4,160,512]{2,1,0:T(8,128)(2,1)S(1)}, bf16[4,160,512]{2,1,0:T(8,128)(2,1)S(1)}, u32[]{:S(2)}, u32[]{:S(2)}) collective-permute-start(bf16[4,160,512]{2,1,0:T(8,128)(2,1)S(1)} %bitcast_select_fusion.4), channel_id=1, source_target_pairs={{0,4},{1,9},{2,6},{3,11},{4,0},{5,13},{6,2},{7,15},{8,12},{9,1},{1... | collective-permute-start | bytes 1966088 | tf_op jit(solution)/shard_map/ppermute | solution.py:698
  177.8 14.5 %collective-permute-start.30 = (bf16[8,56,512]{2,1,0:T(8,128)(2,1)S(1)}, bf16[8,56,512]{2,1,0:T(8,128)(2,1)S(1)}, u32[]{:S(2)}, u32[]{:S(2)}) collective-permute-start(bf16[8,56,512]{2,1,0:T(8,128)(2,1)S(1)} %constant_dynamic-slice_fusion.2.refs_10_), channel_id=1, source_target_pairs={{0,2},{1,5},{2,0},{3,7},{4,6},{5,1},{6,4},{7,3},{8,10},{9,13},{10,... | collective-permute-start | bytes 1376264 | tf_op jit(solution)/shard_map/ppermute | solution.py:685
  192.3 30.2 %collective-permute-start.37 = (bf16[8,160,512]{2,1,0:T(8,128)(2,1)S(1)}, bf16[8,160,512]{2,1,0:T(8,128)(2,1)}, u32[]{:S(2)}, u32[]{:S(2)}) collective-permute-start(bf16[8,160,512]{2,1,0:T(8,128)(2,1)S(1)} %bitcast_select_fusion), channel_id=1, source_target_pairs={{0,2},{1,5},{2,0},{3,7},{4,6},{5,1},{6,4},{7,3},{8,10},{9,13},{10,... | collective-permute-start | bytes 3932168 | tf_op jit(solution)/shard_map/ppermute | solution.py:698
  219.1 13.6 %collective-permute-start.43 = (bf16[8,80,512]{2,1,0:T(8,128)(2,1)}, bf16[8,80,512]{2,1,0:T(8,128)(2,1)}, u32[]{:S(2)}, u32[]{:S(2)}) collective-permute-start(bf16[8,80,512]{2,1,0:T(8,128)(2,1)} %bitcast_select_fusion.2), channel_id=1, source_target_pairs={{0,2},{1,5},{2,0},{3,7},{4,6},{5,1},{6,4},{7,3},{8,10},{9,13},{10,... | collective-permute-start | bytes 1966088 | tf_op jit(solution)/shard_map/ppermute | solution.py:698
  (63 other events, 539.0 us)
